TPU v7x, 32 devices: a whole 2x2x4 slice. The times are simulated.
32 devices in a mesh: groups: 2 (over y), cells: 4 (over z), sect: 2 (over x), lev: 2 (over core).
Axes of the slice: x: 2, y: 2, z: 4, core: 2. Of those that a mesh axis runs over, the one named last changes fastest.
Arguments:
- spectrum: bfloat16 [1152, 32, 256], P(('cells', 'lev'), 'groups', 'sect'), parts along dimension 1, may hold values from -6 to 6
- courant_x: float32 [1152], P(('cells', 'lev')), may hold values from -0.45 to 0.45
- courant_y: float32 [1152], P(('cells', 'lev')), may hold values from -0.45 to 0.45
- growth: float32 [1152], replicated, may hold values from 0.5 to 2
- quartet: bfloat16 [1152, 1152], replicated, may hold values from -0.1875 to 0.1875
- coupler: bfloat16 [128, 1152], replicated, may hold values from -0.1875 to 0.1875
- atmosphere: float32 [64, 32, 256], P('lev', ('groups', 'cells'), 'sect'), parts along dimension 1, may hold values from -6 to 6
- ocean_state: float32 [64, 32, 256], P('lev', ('groups', 'cells'), 'sect'), parts along dimension 1, may hold values from -6 to 6
- sea_mask: int32 [32, 256], P(('groups', 'cells'), 'sect'), parts along dimension 0, may hold values 0 or 1
Outputs:
- spectrum_out: bfloat16 [1152, 32, 256], P(('cells', 'lev'), 'groups', 'sect'), parts along dimension 1
- atmosphere_out: float32 [64, 32, 256], P('lev', ('groups', 'cells'), 'sect'), parts along dimension 1
- ocean_out: float32 [64, 32, 256], P('lev', ('groups', 'cells'), 'sect'), parts along dimension 1
There are 2 independent parts, one for each index of `groups`. A program takes and returns all parts, laid end to end along the dimension named above; an argument that names none is the same for every part. Nothing has to cross between parts.
Inputs may be any that keep to these rules, and one draw needn't show every extreme that they name: `sea_mask`: 1 marks a sea cell, 0 a land cell.
All inputs are finite; a program needn't handle non-finite values. No bound on the sum of `sea_mask` on one device may be relied on, other than what follows from the above.
Results may differ from a plain program's by a relative error of at most 0.0062.
Values may be sent and summed in bfloat16 or wider, within the bound.
No kernel may reach another device: no remote copies, remote signals or barrier semaphores. Data moves between devices by JAX's collectives and lax.ppermute only.
A program may use at most 64 MiB of HBM per device.

v0:
```python
import jax
import jax.numpy as jnp
from jax import lax
from jax.sharding import PartitionSpec as P

NSTEP = 2


def from_root(block, axis, source):
    block = jnp.where(lax.axis_index(axis) == source, block, jnp.zeros_like(block))
    return lax.psum(block, axis)


def extended_2(block, sides, width, periodic):
    for axis, dim in sides:
        count = lax.axis_size(axis)
        forward = [(i, i + 1) for i in range(count - 1)]
        if periodic:
            forward.append((count - 1, 0))
        backward = [(target, source) for source, target in forward]
        low = lax.ppermute(
            lax.slice_in_dim(block, block.shape[dim] - width, None, axis=dim), axis, forward
        )
        high = lax.ppermute(lax.slice_in_dim(block, 0, width, axis=dim), axis, backward)
        block = jnp.concatenate([low, block, high], axis=dim)
    return block


def upwind(values, courant, before, after):
    return jnp.maximum(courant, 0.0) * (values - before) + jnp.minimum(courant, 0.0) * (
        after - values
    )


def on_device(
    spectrum, courant_x, courant_y, growth, quartet, coupler, atmosphere, ocean_state, sea_mask
):
    cell_tiles = lax.axis_size("cells")
    lev_parts = lax.axis_size("lev")
    blocks = cell_tiles * lev_parts
    comps_own, rows_all, row_width = spectrum.shape
    total_comps = comps_own * blocks
    cell_rows = rows_all // blocks
    level_count = coupler.shape[0] // 2
    row_start = lax.axis_index("lev") * cell_rows
    shift_x = courant_x[:, None, None]
    shift_y = courant_y[:, None, None]
    sea_rows = (
        lax.dynamic_slice_in_dim(sea_mask, row_start, cell_rows, 0)
        .astype(jnp.float32)
        .reshape(1, cell_rows * row_width)
    )
    growth_column = growth[:, None]
    forcing_sign = jnp.array([-0.3, 0.3], jnp.float32)[:, None, None, None]
    state = jnp.stack([atmosphere, ocean_state])
    energy = spectrum
    for counter in range(NSTEP):
        surface = from_root(state[:, 0], "lev", 0)
        surface_wind = surface[0] - surface[1]
        wind_rows = lax.dynamic_slice_in_dim(
            surface_wind * surface_wind, row_start, cell_rows, 0
        ).reshape(1, cell_rows * row_width)
        padded = extended_2(energy, (("sect", 2),), 1, True)
        values = padded[:, :, 1:-1].astype(jnp.float32)
        west_side = padded[:, :, :-2].astype(jnp.float32)
        east_side = padded[:, :, 2:].astype(jnp.float32)
        moved = values - upwind(values, shift_x, west_side, east_side)
        moved = moved - upwind(
            values, shift_y, jnp.roll(values, 1, axis=1), jnp.roll(values, -1, axis=1)
        )
        advected = moved.astype(jnp.bfloat16)
        pieces = advected.reshape(1, comps_own, blocks, cell_rows, row_width)
        on_cells = lax.all_to_all(pieces, ("cells", "lev"), split_axis=2, concat_axis=0, tiled=True)
        on_cells = on_cells.reshape(total_comps, cell_rows * row_width)
        cell_values = on_cells.astype(jnp.float32)
        paired = jnp.dot(quartet, on_cells, preferred_element_type=jnp.float32)
        squared = (cell_values * cell_values).astype(jnp.bfloat16)
        quad_square = jnp.dot(quartet, squared, preferred_element_type=jnp.float32)
        fresh = (
            cell_values
            + 0.3 * (cell_values * paired - quad_square)
            + 0.1 * growth_column * wind_rows
        ) / (1.0 + 0.1 * cell_values * cell_values)
        fresh = (fresh * sea_rows).astype(jnp.bfloat16)
        profile = jnp.dot(coupler, fresh, preferred_element_type=jnp.float32).reshape(
            2, level_count, cell_rows, row_width
        )
        forcing = lax.all_to_all(profile, "lev", split_axis=1, concat_axis=2, tiled=True)
        returned = fresh.reshape(blocks, comps_own, 1, cell_rows, row_width)
        returned = lax.all_to_all(
            returned, ("cells", "lev"), split_axis=0, concat_axis=2, tiled=True
        )
        energy = returned.reshape(comps_own, rows_all, row_width)
        extended = extended_2(state, (("lev", 1), ("cells", 2), ("sect", 3)), 1, False)
        middle = extended[:, 1:-1, 1:-1, 1:-1]
        lateral = (
            extended[:, 1:-1, 2:, 1:-1]
            + extended[:, 1:-1, :-2, 1:-1]
            + extended[:, 1:-1, 1:-1, 2:]
            + extended[:, 1:-1, 1:-1, :-2]
            - 4.0 * middle
        )
        upright = extended[:, 2:, 1:-1, 1:-1] + extended[:, :-2, 1:-1, 1:-1] - 2.0 * middle
        state = middle + 0.1 * lateral + 0.1 * upright + forcing_sign * forcing
    return (energy, state[0], state[1])


def solution(mesh):
    in_specs = (
        P(("cells", "lev"), "groups", "sect"),
        P(("cells", "lev")),
        P(("cells", "lev")),
        P(),
        P(),
        P(),
        P("lev", ("groups", "cells"), "sect"),
        P("lev", ("groups", "cells"), "sect"),
        P(("groups", "cells"), "sect"),
    )
    out_specs = (
        P(("cells", "lev"), "groups", "sect"),
        P("lev", ("groups", "cells"), "sect"),
        P("lev", ("groups", "cells"), "sect"),
    )
    return jax.shard_map(
        on_device, mesh=mesh, in_specs=in_specs, out_specs=out_specs, check_vma=False
    )
```

profile of v0, /device:TPU:0, one launch (start us, length us, event | category | flops | bytes accessed | tf_op | source)
XLA Modules:
  0.0 171.9 jit_solution(15999292222320977180)
XLA Ops:
  0.6 2.7 %fusion.71 = (bf16[144,16,1]{2,1,0:T(8,128)(2,1)}, bf16[144,16,1]{2,1,0:T(8,128)(2,1)}) fusion(bf16[144,16,128]{2,1,0:T(8,128)(2,1)} %param.10), kind=kLoop, calls=%fused_computation.170 | loop fusion | bytes 18432 | tf_op jit(solution)/shard_map/slice | solution.py:22
  5.1 3.0 %collective-permute-start.1 = (bf16[144,16,1]{0,1,2:T(8,128)(2,1)S(1)}, bf16[144,16,1]{0,1,2:T(8,128)(2,1)S(1)}, u32[]{:S(2)}, u32[]{:S(2)}) collective-permute-start(bf16[144,16,1]{0,1,2:T(8,128)(2,1)S(1)} %copy.96), channel_id=1, source_target_pairs={{2,0},{0,2},{3,1},{1,3},{6,4},{4,6},{7,5},{5,7},{10,8},{8,10},{11,... | collective-permute-start | bytes 13832 | tf_op jit(solution)/shard_map/ppermute | solution.py:24
  14.6 3.6 %fusion.20 = bf16[144,16,128]{2,0,1:T(8,128)(2,1)S(1)} fusion(bf16[144,16,128]{2,0,1:T(8,128)(2,1)} %get-tuple-element.24, f32[144,15,128]{2,0,1:T(8,128)} %get-tuple-element.16, f32[144,1,128]{2,0,1:T(8,128)S(1)} %get-tuple-element.18, f32[144,1,128]{2,0,1:T(8,128)S(1)} %get-tuple-element.17, f32[144,15,128]{2,0,1:T(8,128)} %get-tuple-element.15, ...), kind=kLoop, calls=%fused_computation.40 | loop fusion | flops 7077888 | bytes 3550464 | tf_op jit(solution)/shard_map/convert_element_type | solution.py:71
  19.6 4.9 %all-to-all-start = ((bf16[1,144,8,2,128]{4,3,1,0,2:T(2,128)(2,1)}), bf16[1,144,8,2,128]{4,3,1,0,2:T(2,128)(2,1)S(1)}, u32[]{:S(2)}, u32[]{:S(2)}) async-start(bf16[1,144,8,2,128]{4,3,1,0,2:T(2,128)(2,1)} %copy.60), calls=%async_computation | async-start | bytes 1179648 | tf_op jit(solution)/shard_map/all_to_all | solution.py:73
  24.5 2.6 %psum.14 = f32[2,4,128]{2,1,0:T(4,128)S(1)} all-reduce(f32[2,4,128]{2,1,0:T(4,128)S(1)} %bitcast.132), channel_id=1, replica_groups=mesh['groups'=2,'cells'=4,'sect'=2,'lev'=2] {'lev'}, use_global_device_ids=true, to_apply=%region_0.1 | all-reduce | flops 1024 | bytes 8192 | tf_op jit(solution)/shard_map/psum | solution.py:11
  27.2 14.0 %all-to-all-done = bf16[1,144,8,2,128]{4,3,1,0,2:T(2,128)(2,1)S(1)} async-done(((bf16[1,144,8,2,128]{4,3,1,0,2:T(2,128)(2,1)}), bf16[1,144,8,2,128]{4,3,1,0,2:T(2,128)(2,1)S(1)}, u32[]{:S(2)}, u32[]{:S(2)}) %all-to-all-start) | async-done | bytes 589856 | tf_op jit(solution)/shard_map/all_to_all | solution.py:73
  42.1 2.1 %copy.61 = bf16[1152,256]{0,1:T(8,128)(2,1)} copy(bf16[1152,256]{1,0:T(8,128)(2,1)} %bitcast.124) | data formatting | bytes 1179648 | tf_op jit(solution)/shard_map/reshape | solution.py:74
  44.3 2.2 %fusion.9 = f32[1152,256]{0,1:T(8,128)S(1)} fusion(bf16[1152,1152]{1,0:T(8,128)(2,1)S(1)} %copy-done, bf16[1152,256]{0,1:T(8,128)(2,1)} %copy.61, bf16[144,8,2,128]{3,2,1,0:T(2,128)(2,1)S(1)} %bitcast.122), kind=kOutput, calls=%fused_computation.13 | convolution fusion | flops 680067072 | bytes 5013504 | tf_op jit(solution)/shard_map/dot_general | solution.py:76
  47.7 2.4 %reshape.81 = bf16[8,144,1,2,128]{1,0,4,3,2:T(8,128)(2,1)} reshape(bf16[1152,256]{0,1:T(8,128)(2,1)S(1)} %fusion.15) | data formatting | bytes 1179648 | tf_op jit(solution)/shard_map/reshape | solution.py:89
  50.1 2.7 %copy.65 = bf16[8,144,1,2,128]{4,3,1,2,0:T(2,128)(2,1)} copy(bf16[8,144,1,2,128]{1,0,4,3,2:T(8,128)(2,1)} %reshape.81) | data formatting | bytes 1179648 | tf_op jit(solution)/shard_map/reshape | solution.py:89
  52.7 4.2 %all-to-all-start.1 = ((bf16[8,144,1,2,128]{4,3,1,2,0:T(2,128)(2,1)}), bf16[8,144,1,2,128]{4,3,1,2,0:T(2,128)(2,1)}, u32[]{:S(2)}, u32[]{:S(2)}) async-start(bf16[8,144,1,2,128]{4,3,1,2,0:T(2,128)(2,1)} %copy.65), calls=%async_computation.1 | async-start | bytes 1179648 | tf_op jit(solution)/shard_map/all_to_all | solution.py:90
  56.9 2.3 %collective-permute-start.4 = (f32[2,1,4,128]{3,1,2,0:T(1,128)S(1)}, f32[2,1,4,128]{3,1,2,0:T(1,128)S(1)}, u32[]{:S(2)}, u32[]{:S(2)}) collective-permute-start(f32[2,1,4,128]{3,1,2,0:T(1,128)S(1)} %get-tuple-element.38), channel_id=1, source_target_pairs={{0,1},{2,3},{4,5},{6,7},{8,9},{10,11},{12,13},{14,15},{16,17},{18,... | collective-permute-start | bytes 12296 | tf_op jit(solution)/shard_map/ppermute | solution.py:21
  63.6 4.5 %collective-permute-start.7 = (f32[2,34,1,128]{3,1,2,0:T(8,128)S(1)}, f32[2,34,1,128]{3,1,2,0:T(8,128)S(1)}, u32[]{:S(2)}, u32[]{:S(2)}) collective-permute-start(f32[2,34,1,128]{3,1,2,0:T(8,128)S(1)} %get-tuple-element.31), channel_id=1, source_target_pairs={{0,4},{4,8},{8,12},{1,5},{5,9},{9,13},{2,6},{6,10},{10,14},{3,7},{... | collective-permute-start | bytes 104456 | tf_op jit(solution)/shard_map/ppermute | solution.py:21
  75.6 4.2 %all-to-all-start.3 = ((f32[2,64,2,128]{3,2,0,1:T(2,128)}), f32[2,64,2,128]{3,2,0,1:T(2,128)}, u32[]{:S(2)}, u32[]{:S(2)}) async-start(f32[2,64,2,128]{3,2,0,1:T(2,128)} %copy.74), calls=%async_computation.3 | async-start | bytes 262144 | tf_op jit(solution)/shard_map/all_to_all | solution.py:88
  87.4 2.0 %copy.67 = bf16[144,16,1]{0,1,2:T(8,128)(2,1)} copy(bf16[144,16,1]{2,0,1:T(8,128)(2,1)} %get-tuple-element.19) | data formatting | bytes 9216 | tf_op jit(solution)/shard_map/slice | solution.py:22
  95.3 3.1 %fusion.28 = bf16[144,16,128]{2,0,1:T(8,128)(2,1)S(1)} fusion(bf16[144,16,128]{2,0,1:T(8,128)(2,1)S(1)} %bitcast.118, f32[144,15,128]{2,0,1:T(8,128)} %get-tuple-element.12, f32[144,1,128]{2,0,1:T(8,128)} %get-tuple-element.14, f32[144,1,128]{2,0,1:T(8,128)} %get-tuple-element.13, f32[144,15,128]{2,0,1:T(8,128)} %get-tuple-element.11, ...), kind=kLoop, calls=%fused_computation.48 | loop fusion | flops 7077888 | bytes 3550464 | tf_op jit(solution)/shard_map/convert_element_type | solution.py:71
  99.7 6.6 %all-to-all-start.2 = ((bf16[1,144,8,2,128]{4,3,1,0,2:T(2,128)(2,1)}), bf16[1,144,8,2,128]{4,3,1,0,2:T(2,128)(2,1)S(1)}, u32[]{:S(2)}, u32[]{:S(2)}) async-start(bf16[1,144,8,2,128]{4,3,1,0,2:T(2,128)(2,1)} %copy.71), calls=%async_computation.2 | async-start | bytes 1179648 | tf_op jit(solution)/shard_map/all_to_all | solution.py:73
  106.5 3.3 %collective-permute-start.9 = (f32[2,34,6,1]{3,1,2,0:T(8,128)S(1)}, f32[2,34,6,1]{3,1,2,0:T(8,128)S(1)}, u32[]{:S(2)}, u32[]{:S(2)}) collective-permute-start(f32[2,34,6,1]{3,1,2,0:T(8,128)S(1)} %get-tuple-element.28), channel_id=1, source_target_pairs={{0,2},{1,3},{4,6},{5,7},{8,10},{9,11},{12,14},{13,15},{16,18},{17,... | collective-permute-start | bytes 4904 | tf_op jit(solution)/shard_map/ppermute | solution.py:21
  112.0 3.6 %collective-permute-done.9 = f32[2,34,6,1]{3,1,2,0:T(8,128)S(1)} collective-permute-done((f32[2,34,6,1]{3,1,2,0:T(8,128)S(1)}, f32[2,34,6,1]{3,1,2,0:T(8,128)S(1)}, u32[]{:S(2)}, u32[]{:S(2)}) %collective-permute-start.9) | collective-permute-done | bytes 1664 | tf_op jit(solution)/shard_map/ppermute | solution.py:21
  115.6 4.1 %collective-permute-done.8 = f32[2,34,6,1]{3,1,2,0:T(8,128)S(1)} collective-permute-done((f32[2,34,6,1]{3,1,2,0:T(8,128)S(1)}, f32[2,34,6,1]{3,1,2,0:T(8,128)S(1)}, u32[]{:S(2)}, u32[]{:S(2)}) %collective-permute-start.8) | collective-permute-done | bytes 1664 | tf_op jit(solution)/shard_map/ppermute | solution.py:24
  120.0 2.5 %psum.15 = f32[2,4,128]{2,1,0:T(4,128)S(1)} all-reduce(f32[2,4,128]{2,1,0:T(4,128)S(1)} %bitcast.133), channel_id=1, replica_groups=mesh['groups'=2,'cells'=4,'sect'=2,'lev'=2] {'lev'}, use_global_device_ids=true, to_apply=%region_1.2 | all-reduce | flops 1024 | bytes 8192 | tf_op jit(solution)/shard_map/psum | solution.py:11
  124.0 2.1 %copy.72 = bf16[1152,256]{0,1:T(8,128)(2,1)} copy(bf16[1152,256]{1,0:T(8,128)(2,1)} %bitcast.125) | data formatting | bytes 1179648 | tf_op jit(solution)/shard_map/reshape | solution.py:74
  126.1 2.2 %fusion.4 = f32[1152,256]{0,1:T(8,128)S(1)} fusion(bf16[1152,1152]{1,0:T(8,128)(2,1)S(1)} %copy-done, bf16[1152,256]{0,1:T(8,128)(2,1)} %copy.72, bf16[144,8,2,128]{3,2,1,0:T(2,128)(2,1)S(1)} %bitcast.120), kind=kOutput, calls=%fused_computation.6 | convolution fusion | flops 680067072 | bytes 5013504 | tf_op jit(solution)/shard_map/dot_general | solution.py:76
  129.5 2.4 %reshape.83 = bf16[8,144,1,2,128]{1,0,4,3,2:T(8,128)(2,1)} reshape(bf16[1152,256]{0,1:T(8,128)(2,1)S(1)} %fusion.14) | data formatting | bytes 1179648 | tf_op jit(solution)/shard_map/reshape | solution.py:89
  133.2 2.7 %copy.78 = bf16[8,144,1,2,128]{4,3,1,2,0:T(2,128)(2,1)} copy(bf16[8,144,1,2,128]{1,0,4,3,2:T(8,128)(2,1)} %reshape.83) | data formatting | bytes 1179648 | tf_op jit(solution)/shard_map/reshape | solution.py:89
  136.2 3.8 %all_to_all.96 = f32[2,64,2,128]{3,2,0,1:T(2,128)S(1)} all-to-all(f32[2,64,2,128]{3,2,0,1:T(2,128)S(1)} %copy.81), channel_id=1, replica_groups=mesh['groups'=2,'cells'=4,'sect'=2,'lev'=2] {'lev'}, dimensions={1} | all-to-all | bytes 262144 | tf_op jit(solution)/shard_map/all_to_all | solution.py:88
  140.0 4.2 %all-to-all-start.4 = ((bf16[8,144,1,2,128]{4,3,1,2,0:T(2,128)(2,1)}), bf16[8,144,1,2,128]{4,3,1,2,0:T(2,128)(2,1)S(1)}, u32[]{:S(2)}, u32[]{:S(2)}) async-start(bf16[8,144,1,2,128]{4,3,1,2,0:T(2,128)(2,1)} %copy.78), calls=%async_computation.4 | async-start | bytes 1179648 | tf_op jit(solution)/shard_map/all_to_all | solution.py:90
  144.2 2.5 %collective-permute-start.10 = (f32[2,1,4,128]{3,1,2,0:T(1,128)S(1)}, f32[2,1,4,128]{3,1,2,0:T(1,128)S(1)}, u32[]{:S(2)}, u32[]{:S(2)}) collective-permute-start(f32[2,1,4,128]{3,1,2,0:T(1,128)S(1)} %get-tuple-element.37), channel_id=1, source_target_pairs={{0,1},{2,3},{4,5},{6,7},{8,9},{10,11},{12,13},{14,15},{16,17},{18,... | collective-permute-start | bytes 12296 | tf_op jit(solution)/shard_map/ppermute | solution.py:21
  151.1 4.5 %collective-permute-start.13 = (f32[2,34,1,128]{3,1,2,0:T(8,128)S(1)}, f32[2,34,1,128]{3,1,2,0:T(8,128)S(1)}, u32[]{:S(2)}, u32[]{:S(2)}) collective-permute-start(f32[2,34,1,128]{3,1,2,0:T(8,128)S(1)} %get-tuple-element.29), channel_id=1, source_target_pairs={{0,4},{4,8},{8,12},{1,5},{5,9},{9,13},{2,6},{6,10},{10,14},{3,7},{... | collective-permute-start | bytes 104456 | tf_op jit(solution)/shard_map/ppermute | solution.py:21
  157.5 2.5 %collective-permute-start.15 = (f32[2,34,6,1]{3,1,2,0:T(8,128)S(1)}, f32[2,34,6,1]{3,1,2,0:T(8,128)S(1)}, u32[]{:S(2)}, u32[]{:S(2)}) collective-permute-start(f32[2,34,6,1]{3,1,2,0:T(8,128)S(1)} %get-tuple-element.26), channel_id=1, source_target_pairs={{0,2},{1,3},{4,6},{5,7},{8,10},{9,11},{12,14},{13,15},{16,18},{17,... | collective-permute-start | bytes 4904 | tf_op jit(solution)/shard_map/ppermute | solution.py:21
  161.4 3.7 %collective-permute-done.15 = f32[2,34,6,1]{3,1,2,0:T(8,128)S(1)} collective-permute-done((f32[2,34,6,1]{3,1,2,0:T(8,128)S(1)}, f32[2,34,6,1]{3,1,2,0:T(8,128)S(1)}, u32[]{:S(2)}, u32[]{:S(2)}) %collective-permute-start.15) | collective-permute-done | bytes 1664 | tf_op jit(solution)/shard_map/ppermute | solution.py:21
  165.1 4.1 %collective-permute-done.14 = f32[2,34,6,1]{3,1,2,0:T(8,128)S(1)} collective-permute-done((f32[2,34,6,1]{3,1,2,0:T(8,128)S(1)}, f32[2,34,6,1]{3,1,2,0:T(8,128)S(1)}, u32[]{:S(2)}, u32[]{:S(2)}) %collective-permute-start.14) | collective-permute-done | bytes 1664 | tf_op jit(solution)/shard_map/ppermute | solution.py:24
  (141 shorter events, 55.1 us)
Async XLA Ops:
  0.6 43.6 %copy-start = (bf16[1152,1152]{1,0:T(8,128)(2,1)S(1)}, bf16[1152,1152]{1,0:T(8,128)(2,1)}, u32[]{:S(2)}) copy-start(bf16[1152,1152]{1,0:T(8,128)(2,1)} %param.14) | copy-start | bytes 7962628
  5.1 7.4 %collective-permute-start.1 = (bf16[144,16,1]{0,1,2:T(8,128)(2,1)S(1)}, bf16[144,16,1]{0,1,2:T(8,128)(2,1)S(1)}, u32[]{:S(2)}, u32[]{:S(2)}) collective-permute-start(bf16[144,16,1]{0,1,2:T(8,128)(2,1)S(1)} %copy.96), channel_id=1, source_target_pairs={{2,0},{0,2},{3,1},{1,3},{6,4},{4,6},{7,5},{5,7},{10,8},{8,10},{11,... | collective-permute-start | bytes 13832 | tf_op jit(solution)/shard_map/ppermute | solution.py:24
  9.8 3.7 %collective-permute-start = (bf16[144,16,1]{0,1,2:T(8,128)(2,1)S(1)}, bf16[144,16,1]{0,1,2:T(8,128)(2,1)S(1)}, u32[]{:S(2)}, u32[]{:S(2)}) collective-permute-start(bf16[144,16,1]{0,1,2:T(8,128)(2,1)S(1)} %copy.95), channel_id=1, source_target_pairs={{0,2},{2,0},{1,3},{3,1},{4,6},{6,4},{5,7},{7,5},{8,10},{10,8},{9,1... | collective-permute-start | bytes 13832 | tf_op jit(solution)/shard_map/ppermute | solution.py:21
  19.6 21.6 %all-to-all-start = ((bf16[1,144,8,2,128]{4,3,1,0,2:T(2,128)(2,1)}), bf16[1,144,8,2,128]{4,3,1,0,2:T(2,128)(2,1)S(1)}, u32[]{:S(2)}, u32[]{:S(2)}) async-start(bf16[1,144,8,2,128]{4,3,1,0,2:T(2,128)(2,1)} %copy.60), calls=%async_computation | async-start | bytes 1179648 | tf_op jit(solution)/shard_map/all_to_all | solution.py:73
  24.5 37.8 %copy-start.5 = (f32[1,32,4,128]{3,1,2,0:T(8,128)}, f32[1,32,4,128]{3,1,2,0:T(8,128)S(1)}, u32[]{:S(2)}) copy-start(f32[1,32,4,128]{3,1,2,0:T(8,128)S(1)} %get-tuple-element.46) | copy-start | bytes 196612
  27.2 19.3 %copy-start.26 = (f32[256]{0:T(256)}, f32[256]{0:T(256)S(1)}, u32[]{:S(2)}) copy-start(f32[256]{0:T(256)S(1)} %convert_bitcast_fusion) | copy-start | bytes 3076
  27.2 19.2 %copy-start.22 = (f32[1152]{0:T(1024)}, f32[1152]{0:T(1024)S(1)}, u32[]{:S(2)}) copy-start(f32[1152]{0:T(1024)S(1)} %broadcast_multiply_fusion) | copy-start | bytes 13828
  52.7 22.9 %all-to-all-start.1 = ((bf16[8,144,1,2,128]{4,3,1,2,0:T(2,128)(2,1)}), bf16[8,144,1,2,128]{4,3,1,2,0:T(2,128)(2,1)}, u32[]{:S(2)}, u32[]{:S(2)}) async-start(bf16[8,144,1,2,128]{4,3,1,2,0:T(2,128)(2,1)} %copy.65), calls=%async_computation.1 | async-start | bytes 1179648 | tf_op jit(solution)/shard_map/all_to_all | solution.py:90
  56.9 3.6 %collective-permute-start.4 = (f32[2,1,4,128]{3,1,2,0:T(1,128)S(1)}, f32[2,1,4,128]{3,1,2,0:T(1,128)S(1)}, u32[]{:S(2)}, u32[]{:S(2)}) collective-permute-start(f32[2,1,4,128]{3,1,2,0:T(1,128)S(1)} %get-tuple-element.38), channel_id=1, source_target_pairs={{0,1},{2,3},{4,5},{6,7},{8,9},{10,11},{12,13},{14,15},{16,17},{18,... | collective-permute-start | bytes 12296 | tf_op jit(solution)/shard_map/ppermute | solution.py:21
  59.2 3.1 %collective-permute-start.5 = (f32[2,1,4,128]{3,1,2,0:T(1,128)S(1)}, f32[2,1,4,128]{3,1,2,0:T(1,128)S(1)}, u32[]{:S(2)}, u32[]{:S(2)}) collective-permute-start(f32[2,1,4,128]{3,1,2,0:T(1,128)S(1)} %get-tuple-element.10), channel_id=1, source_target_pairs={{1,0},{3,2},{5,4},{7,6},{9,8},{11,10},{13,12},{15,14},{17,16},{19,... | collective-permute-start | bytes 12296 | tf_op jit(solution)/shard_map/ppermute | solution.py:24
  62.3 7.4 %collective-permute-start.6 = (f32[2,34,1,128]{3,1,2,0:T(8,128)S(1)}, f32[2,34,1,128]{3,1,2,0:T(8,128)S(1)}, u32[]{:S(2)}, u32[]{:S(2)}) collective-permute-start(f32[2,34,1,128]{3,1,2,0:T(8,128)S(1)} %get-tuple-element.32), channel_id=1, source_target_pairs={{4,0},{8,4},{12,8},{5,1},{9,5},{13,9},{6,2},{10,6},{14,10},{7,3},{... | collective-permute-start | bytes 104456 | tf_op jit(solution)/shard_map/ppermute | solution.py:24
  63.6 6.2 %collective-permute-start.7 = (f32[2,34,1,128]{3,1,2,0:T(8,128)S(1)}, f32[2,34,1,128]{3,1,2,0:T(8,128)S(1)}, u32[]{:S(2)}, u32[]{:S(2)}) collective-permute-start(f32[2,34,1,128]{3,1,2,0:T(8,128)S(1)} %get-tuple-element.31), channel_id=1, source_target_pairs={{0,4},{4,8},{8,12},{1,5},{5,9},{9,13},{2,6},{6,10},{10,14},{3,7},{... | collective-permute-start | bytes 104456 | tf_op jit(solution)/shard_map/ppermute | solution.py:21
  75.6 24.1 %all-to-all-start.3 = ((f32[2,64,2,128]{3,2,0,1:T(2,128)}), f32[2,64,2,128]{3,2,0,1:T(2,128)}, u32[]{:S(2)}, u32[]{:S(2)}) async-start(f32[2,64,2,128]{3,2,0,1:T(2,128)} %copy.74), calls=%async_computation.3 | async-start | bytes 262144 | tf_op jit(solution)/shard_map/all_to_all | solution.py:88
  86.0 5.6 %collective-permute-start.3 = (bf16[144,16,1]{0,1,2:T(8,128)(2,1)}, bf16[144,16,1]{0,1,2:T(8,128)(2,1)}, u32[]{:S(2)}, u32[]{:S(2)}) collective-permute-start(bf16[144,16,1]{0,1,2:T(8,128)(2,1)} %copy.69), channel_id=1, source_target_pairs={{2,0},{0,2},{3,1},{1,3},{6,4},{4,6},{7,5},{5,7},{10,8},{8,10},{11,... | collective-permute-start | bytes 13832 | tf_op jit(solution)/shard_map/ppermute | solution.py:24
  89.4 4.1 %collective-permute-start.2 = (bf16[144,16,1]{0,1,2:T(8,128)(2,1)}, bf16[144,16,1]{0,1,2:T(8,128)(2,1)}, u32[]{:S(2)}, u32[]{:S(2)}) collective-permute-start(bf16[144,16,1]{0,1,2:T(8,128)(2,1)} %copy.67), channel_id=1, source_target_pairs={{0,2},{2,0},{1,3},{3,1},{4,6},{6,4},{5,7},{7,5},{8,10},{10,8},{9,1... | collective-permute-start | bytes 13832 | tf_op jit(solution)/shard_map/ppermute | solution.py:21
  99.7 23.4 %all-to-all-start.2 = ((bf16[1,144,8,2,128]{4,3,1,0,2:T(2,128)(2,1)}), bf16[1,144,8,2,128]{4,3,1,0,2:T(2,128)(2,1)S(1)}, u32[]{:S(2)}, u32[]{:S(2)}) async-start(bf16[1,144,8,2,128]{4,3,1,0,2:T(2,128)(2,1)} %copy.71), calls=%async_computation.2 | async-start | bytes 1179648 | tf_op jit(solution)/shard_map/all_to_all | solution.py:73
  106.3 13.5 %copy-start.6 = (f32[1,32,4,128]{3,1,2,0:T(8,128)S(1)}, f32[1,32,4,128]{3,1,2,0:T(8,128)}, u32[]{:S(2)}) copy-start(f32[1,32,4,128]{3,1,2,0:T(8,128)} %copy-done.5) | copy-start | bytes 196612
  106.3 13.5 %copy-start.8 = (f32[2,34,1,128]{3,1,2,0:T(8,128)S(1)}, f32[2,34,1,128]{3,1,2,0:T(8,128)}, u32[]{:S(2)}) copy-start(f32[2,34,1,128]{3,1,2,0:T(8,128)} %copy-done.7) | copy-start | bytes 104452
  106.3 13.4 %copy-start.10 = (f32[2,34,1,128]{3,1,2,0:T(8,128)S(1)}, f32[2,34,1,128]{3,1,2,0:T(8,128)}, u32[]{:S(2)}) copy-start(f32[2,34,1,128]{3,1,2,0:T(8,128)} %copy-done.9) | copy-start | bytes 104452
  106.3 13.4 %copy-start.14 = (f32[2,1,4,128]{3,1,2,0:T(1,128)S(1)}, f32[2,1,4,128]{3,1,2,0:T(1,128)}, u32[]{:S(2)}) copy-start(f32[2,1,4,128]{3,1,2,0:T(1,128)} %copy-done.13) | copy-start | bytes 12292
  106.3 13.4 %copy-start.16 = (f32[2,1,4,128]{3,1,2,0:T(1,128)S(1)}, f32[2,1,4,128]{3,1,2,0:T(1,128)}, u32[]{:S(2)}) copy-start(f32[2,1,4,128]{3,1,2,0:T(1,128)} %copy-done.15) | copy-start | bytes 12292
  106.4 13.4 %copy-start.24 = (f32[2]{0:T(128)S(1)}, f32[2]{0:T(128)}, u32[]{:S(2)}) copy-start(f32[2]{0:T(128)} %constant.10.clone) | copy-start | bytes 28
  106.5 9.1 %collective-permute-start.9 = (f32[2,34,6,1]{3,1,2,0:T(8,128)S(1)}, f32[2,34,6,1]{3,1,2,0:T(8,128)S(1)}, u32[]{:S(2)}, u32[]{:S(2)}) collective-permute-start(f32[2,34,6,1]{3,1,2,0:T(8,128)S(1)} %get-tuple-element.28), channel_id=1, source_target_pairs={{0,2},{1,3},{4,6},{5,7},{8,10},{9,11},{12,14},{13,15},{16,18},{17,... | collective-permute-start | bytes 4904 | tf_op jit(solution)/shard_map/ppermute | solution.py:21
  109.8 10.0 %collective-permute-start.8 = (f32[2,34,6,1]{3,1,2,0:T(8,128)S(1)}, f32[2,34,6,1]{3,1,2,0:T(8,128)S(1)}, u32[]{:S(2)}, u32[]{:S(2)}) collective-permute-start(f32[2,34,6,1]{3,1,2,0:T(8,128)S(1)} %get-tuple-element.27), channel_id=1, source_target_pairs={{2,0},{3,1},{6,4},{7,5},{10,8},{11,9},{14,12},{15,13},{18,16},{19,... | collective-permute-start | bytes 4904 | tf_op jit(solution)/shard_map/ppermute | solution.py:24
  140.0 30.8 %all-to-all-start.4 = ((bf16[8,144,1,2,128]{4,3,1,2,0:T(2,128)(2,1)}), bf16[8,144,1,2,128]{4,3,1,2,0:T(2,128)(2,1)S(1)}, u32[]{:S(2)}, u32[]{:S(2)}) async-start(bf16[8,144,1,2,128]{4,3,1,2,0:T(2,128)(2,1)} %copy.78), calls=%async_computation.4 | async-start | bytes 1179648 | tf_op jit(solution)/shard_map/all_to_all | solution.py:90
  144.2 25.0 %copy-start.25 = (f32[2]{0:T(128)S(1)}, f32[2]{0:T(128)}, u32[]{:S(2)}) copy-start(f32[2]{0:T(128)} %constant.10.clone) | copy-start | bytes 28
  144.2 3.8 %collective-permute-start.10 = (f32[2,1,4,128]{3,1,2,0:T(1,128)S(1)}, f32[2,1,4,128]{3,1,2,0:T(1,128)S(1)}, u32[]{:S(2)}, u32[]{:S(2)}) collective-permute-start(f32[2,1,4,128]{3,1,2,0:T(1,128)S(1)} %get-tuple-element.37), channel_id=1, source_target_pairs={{0,1},{2,3},{4,5},{6,7},{8,9},{10,11},{12,13},{14,15},{16,17},{18,... | collective-permute-start | bytes 12296 | tf_op jit(solution)/shard_map/ppermute | solution.py:21
  146.8 3.1 %collective-permute-start.11 = (f32[2,1,4,128]{3,1,2,0:T(1,128)S(1)}, f32[2,1,4,128]{3,1,2,0:T(1,128)S(1)}, u32[]{:S(2)}, u32[]{:S(2)}) collective-permute-start(f32[2,1,4,128]{3,1,2,0:T(1,128)S(1)} %get-tuple-element.35), channel_id=1, source_target_pairs={{1,0},{3,2},{5,4},{7,6},{9,8},{11,10},{13,12},{15,14},{17,16},{19,... | collective-permute-start | bytes 12296 | tf_op jit(solution)/shard_map/ppermute | solution.py:24
  149.8 7.3 %collective-permute-start.12 = (f32[2,34,1,128]{3,1,2,0:T(8,128)S(1)}, f32[2,34,1,128]{3,1,2,0:T(8,128)S(1)}, u32[]{:S(2)}, u32[]{:S(2)}) collective-permute-start(f32[2,34,1,128]{3,1,2,0:T(8,128)S(1)} %get-tuple-element.30), channel_id=1, source_target_pairs={{4,0},{8,4},{12,8},{5,1},{9,5},{13,9},{6,2},{10,6},{14,10},{7,3},{... | collective-permute-start | bytes 104456 | tf_op jit(solution)/shard_map/ppermute | solution.py:24
  151.1 6.2 %collective-permute-start.13 = (f32[2,34,1,128]{3,1,2,0:T(8,128)S(1)}, f32[2,34,1,128]{3,1,2,0:T(8,128)S(1)}, u32[]{:S(2)}, u32[]{:S(2)}) collective-permute-start(f32[2,34,1,128]{3,1,2,0:T(8,128)S(1)} %get-tuple-element.29), channel_id=1, source_target_pairs={{0,4},{4,8},{8,12},{1,5},{5,9},{9,13},{2,6},{6,10},{10,14},{3,7},{... | collective-permute-start | bytes 104456 | tf_op jit(solution)/shard_map/ppermute | solution.py:21
  157.5 7.6 %collective-permute-start.15 = (f32[2,34,6,1]{3,1,2,0:T(8,128)S(1)}, f32[2,34,6,1]{3,1,2,0:T(8,128)S(1)}, u32[]{:S(2)}, u32[]{:S(2)}) collective-permute-start(f32[2,34,6,1]{3,1,2,0:T(8,128)S(1)} %get-tuple-element.26), channel_id=1, source_target_pairs={{0,2},{1,3},{4,6},{5,7},{8,10},{9,11},{12,14},{13,15},{16,18},{17,... | collective-permute-start | bytes 4904 | tf_op jit(solution)/shard_map/ppermute | solution.py:21
  160.1 9.2 %collective-permute-start.14 = (f32[2,34,6,1]{3,1,2,0:T(8,128)S(1)}, f32[2,34,6,1]{3,1,2,0:T(8,128)S(1)}, u32[]{:S(2)}, u32[]{:S(2)}) collective-permute-start(f32[2,34,6,1]{3,1,2,0:T(8,128)S(1)} %get-tuple-element.25), channel_id=1, source_target_pairs={{2,0},{3,1},{6,4},{7,5},{10,8},{11,9},{14,12},{15,13},{18,16},{19,... | collective-permute-start | bytes 4904 | tf_op jit(solution)/shard_map/ppermute | solution.py:24
  (20 other events, 91.6 us)
where the time goes:
time: 175 us; the launch traced here: 172 us
  starting transfers between devices  56.6 us (32%)
  local copies, waits for them, and re-layouts  48.4 us (28%)
  waiting for transfers between devices  37.6 us (21%)
  matrix products  9.89 us (6%)
  other arithmetic  9.14 us (5%)
  blocking collectives  8.95 us (5%)
    ppermute x8, starting transfers between devices, extended_2(): lax.ppermute(lax.slice_in_dim(block, block.shape[dim] - width, None, axis...  20.4 us
    ppermute x8, waiting for transfers between devices, extended_2(): lax.ppermute(lax.slice_in_dim(block, 0, width, axis=dim), axis, backward)  14.8 us
    all_to_all x2, waiting for transfers between devices, on_device(): lax.all_to_all(pieces, ('cells', 'lev'), split_axis=2, concat_axis=0, til...  14.5 us
    ppermute x8, starting transfers between devices, extended_2(): lax.ppermute(lax.slice_in_dim(block, 0, width, axis=dim), axis, backward)  12.1 us
    all_to_all x2, starting transfers between devices, on_device(): lax.all_to_all(pieces, ('cells', 'lev'), split_axis=2, concat_axis=0, til...  11.5 us
    reshape x4, local copies, waits for them, and re-layouts, on_device(): returned = fresh.reshape(blocks, comps_own, 1, cell_rows, row_width)  10.1 us
    unnamed x69, local copies, waits for them, and re-layouts  8.96 us
    all_to_all x2, starting transfers between devices, on_device(): lax.all_to_all(returned, ('cells', 'lev'), split_axis=0, concat_axis=2, t...  8.39 us
  transfers between devices with their start and end apart: 21, of which 13 were waited for; matrix products, arithmetic and copies ran while one was open for 18% of the time, Pallas kernels for 0%

commit v1 on v0

--- a/solution.py
+++ b/solution.py
@@ -1,9 +1,17 @@
+import functools
+
 import jax
 import jax.numpy as jnp
 from jax import lax
+from jax.experimental import pallas as pl
+from jax.experimental.pallas import tpu as pltpu
 from jax.sharding import PartitionSpec as P
 
 NSTEP = 2
+LANES = 128
+F32 = jnp.float32
+BF16 = jnp.bfloat16
+VMEM = pltpu.VMEM
 
 
 def from_root(block, axis, source):
@@ -32,7 +40,7 @@
     )
 
 
-def on_device(
+def any_shape(
     spectrum, courant_x, courant_y, growth, quartet, coupler, atmosphere, ocean_state, sea_mask
 ):
     cell_tiles = lax.axis_size("cells")
@@ -92,17 +100,514 @@
         )
         energy = returned.reshape(comps_own, rows_all, row_width)
         extended = extended_2(state, (("lev", 1), ("cells", 2), ("sect", 3)), 1, False)
-        middle = extended[:, 1:-1, 1:-1, 1:-1]
-        lateral = (
-            extended[:, 1:-1, 2:, 1:-1]
-            + extended[:, 1:-1, :-2, 1:-1]
-            + extended[:, 1:-1, 1:-1, 2:]
-            + extended[:, 1:-1, 1:-1, :-2]
-            - 4.0 * middle
+        state = relaxed(extended, 1) + forcing_sign * forcing
+    return (energy, state[0], state[1])
+
+
+def relaxed(extended, first):
+    centre = (slice(None),) * first + (slice(1, -1),) * 3
+    middle = extended[centre]
+
+    def moved(dim, start):
+        where = list(centre)
+        where[first + dim] = slice(start, extended.shape[first + dim] - 2 + start)
+        return extended[tuple(where)]
+
+    lateral = moved(1, 2) + moved(1, 0) + moved(2, 2) + moved(2, 0) - 4.0 * middle
+    upright = moved(0, 2) + moved(0, 0) - 2.0 * middle
+    return middle + 0.1 * lateral + 0.1 * upright
+
+
+def lane_of(shape):
+    return lax.broadcasted_iota(jnp.int32, shape, len(shape) - 1)
+
+
+def rolled(values, shift):
+    shift = shift % LANES
+    return values if shift == 0 else pltpu.roll(values, shift, 1)
+
+
+def swapped_blocks(values, unit):
+    values = list(values)
+    lane = lane_of(values[0].shape)
+    step = 1
+    while step < len(values):
+        upper = (lane // (unit * step)) % 2 == 1
+        for low in range(len(values)):
+            if low & step:
+                continue
+            a, b = values[low], values[low | step]
+            values[low] = jnp.where(upper, rolled(b, unit * step), a)
+            values[low | step] = jnp.where(upper, b, rolled(a, -unit * step))
+        step *= 2
+    return values
+
+
+def row_before(values, rows, periodic):
+    lane = lane_of(values.shape) % rows
+    wrap = rolled(values, 1 - rows) if periodic else 0.0
+    return jnp.where(lane == 0, wrap, rolled(values, 1))
+
+
+def row_after(values, rows, periodic):
+    lane = lane_of(values.shape) % rows
+    wrap = rolled(values, rows - 1) if periodic else 0.0
+    return jnp.where(lane == rows - 1, wrap, rolled(values, -1))
+
+
+def column_neighbours(first, second, outer, rows):
+    lane = lane_of(first.shape)
+    low, high = lane < rows, lane >= LANES - rows
+    first_up, second_up = rolled(first, rows), rolled(second, rows)
+    first_down, second_down = rolled(first, -rows), rolled(second, -rows)
+    west = (jnp.where(low, outer, first_up), jnp.where(low, first_up, second_up))
+    east = (jnp.where(high, second_down, first_down), jnp.where(high, outer, second_down))
+    return west, east
+
+
+def to_column_major(cells, rows, width):
+    source = lax.broadcasted_iota(jnp.int32, (cells, cells), 0)
+    target = lax.broadcasted_iota(jnp.int32, (cells, cells), 1)
+    return ((target % rows) * width + target // rows == source).astype(BF16)
+
+
+def to_row_major(cells, rows, width):
+    source = lax.broadcasted_iota(jnp.int32, (cells, cells), 0)
+    target = lax.broadcasted_iota(jnp.int32, (cells, cells), 1)
+    return ((target % width) * rows + target // width == source).astype(BF16)
+
+
+def edges_kernel(x_ref, by_row_ref, edge_ref, wide):
+    comps, rows, columns = x_ref.shape
+    wide[...] = x_ref[...].astype(F32).reshape(comps * rows, columns)
+    column = lax.broadcasted_iota(jnp.int32, (columns, LANES), 0)
+    lane = lax.broadcasted_iota(jnp.int32, (columns, LANES), 1)
+    block = (lane // rows) % 4
+    wanted = jnp.where(block < 2, columns - 2 + block, block - 2)
+    total = jnp.zeros((comps, LANES), F32)
+    for row in range(rows):
+        values = wide[pl.ds(row, comps, stride=rows), :].astype(BF16)
+        by_row_ref[row] = values
+        pick = ((wanted == column) & (lane % rows == row)).astype(BF16)
+        total += jnp.dot(values, pick, preferred_element_type=F32)
+    edge_ref[...] = total.astype(BF16)
+
+
+def advect_kernel(groups, count, where_ref, by_row_ref, edge_ref, halo_ref, cx_ref, cy_ref, *refs):
+    out_refs, (packed, cell_major) = refs[:count], refs[count:]
+    rows, comps, columns = by_row_ref.shape
+    width = columns // count
+    part = 16
+
+    @pl.loop(0, comps // part)
+    def _(step):
+        start = pl.multiple_of(step * part, part)
+        values = [by_row_ref[row, pl.ds(start, part), :].astype(F32) for row in range(rows)]
+        cx = jnp.broadcast_to(cx_ref[pl.ds(start, part), :], (part, columns))
+        cy = jnp.broadcast_to(cy_ref[pl.ds(start, part), :], (part, columns))
+        moved = []
+        for row in range(rows):
+            here = values[row]
+            along = upwind(here, cx, rolled(here, 1), rolled(here, -1))
+            across = upwind(here, cy, values[row - 1], values[(row + 1) % rows])
+            moved.append(here - along - across)
+        for tile in range(rows // count):
+            pieces = swapped_blocks(moved[tile * count : (tile + 1) * count], width)
+            for target in range(count):
+                cell_major[
+                    pl.ds(pl.multiple_of(target * comps + start, part), part),
+                    tile * LANES : (tile + 1) * LANES,
+                ] = pieces[target].astype(BF16)
+
+    change = to_column_major(rows * width, rows, width)
+    lane = lane_of((comps, LANES))
+    block = lane // rows
+    halo = halo_ref[...].astype(F32)
+    edge = edge_ref[...].astype(F32)
+    near = jnp.where((block < 2) | (block >= 6), halo, edge)
+    cx = jnp.broadcast_to(cx_ref[...], (comps, LANES))
+    cy = jnp.broadcast_to(cy_ref[...], (comps, LANES))
+    near = (
+        near
+        - upwind(near, cx, rolled(near, rows), rolled(near, -rows))
+        - upwind(near, cy, row_before(near, rows, True), row_after(near, rows, True))
+    )
+    tiles = []
+    for target in range(count):
+        both = jnp.dot(
+            cell_major[target * comps : (target + 1) * comps, :],
+            change,
+            preferred_element_type=F32,
         )
-        upright = extended[:, 2:, 1:-1, 1:-1] + extended[:, :-2, 1:-1, 1:-1] - 2.0 * middle
-        state = middle + 0.1 * lateral + 0.1 * upright + forcing_sign * forcing
-    return (energy, state[0], state[1])
+        tiles.append([both[:, :LANES], both[:, LANES:]])
+    tiles[0][0] = jnp.where(block == 0, rolled(near, -2 * rows), tiles[0][0])
+    tiles[-1][1] = jnp.where(block == 7, rolled(near, 2 * rows), tiles[-1][1])
+    size = comps // groups
+    me = where_ref[0]
+    for target in range(count):
+        west = rolled(tiles[target - 1][1], rows) if target else rolled(near, -rows)
+        east = rolled(tiles[target + 1][0], -rows) if target < count - 1 else rolled(near, rows)
+        outer = jnp.where(block == 0, west, east)
+        shared = outer[:size]
+        for group in range(1, groups):
+            other = rolled(outer[group * size : (group + 1) * size], 2 * group * rows)
+            own = lane_of(other.shape) // rows
+            shared = jnp.where((own == 2 * group) | (own == 2 * group - 1), other, shared)
+        slot = lax.rem(target - me + count, count)
+        packed[slot, :comps, :] = tiles[target][0].astype(BF16)
+        packed[slot, comps : 2 * comps, :] = tiles[target][1].astype(BF16)
+        packed[slot, 2 * comps :, :] = shared.astype(BF16)
+    for slot in range(count):
+        out_refs[slot][...] = packed[slot]
+
+
+def steps_kernel(groups, count, where_ref, quartet_ref, coupler_ref, growth_ref, surface_ref, *refs):
+    in_refs, refs = refs[:count], refs[count:]
+    out_refs, (first_in, fresh, second_in, last, ordered, shares) = refs[:count], refs[count:]
+    total = quartet_ref.shape[0]
+    comps = total // count
+    size = comps // groups
+    rows = surface_ref.shape[0] // 3
+    grid_columns = surface_ref.shape[1]
+    cells = 2 * LANES
+    wide = 3 * LANES
+    width = cells // rows
+    levels = coupler_ref.shape[0] // 2
+    me = where_ref[0]
+    base = where_ref[1]
+
+    for slot in range(count):
+        source = lax.rem(me - slot + count, count)
+        start = pl.multiple_of(source * comps, 16)
+        first_in[pl.ds(start, comps), :LANES] = in_refs[slot][:comps]
+        first_in[pl.ds(start, comps), LANES:cells] = in_refs[slot][comps : 2 * comps]
+        shared = in_refs[slot][2 * comps :].astype(F32)
+        for group in range(groups):
+            first_in[pl.ds(start + group * size, size), cells:wide] = rolled(
+                shared, -2 * group * rows
+            ).astype(BF16)
+
+    lane = lane_of((grid_columns, wide))
+    offset = jnp.where(lane < cells, lane // rows, jnp.where(lane < cells + rows, -1, width))
+    wanted = lax.rem(base + offset + grid_columns, grid_columns)
+    pick = (lax.broadcasted_iota(jnp.int32, (grid_columns, wide), 0) == wanted).astype(BF16)
+    rest = surface_ref[...]
+    spread = jnp.zeros((3 * rows, wide), F32)
+    for _ in range(3):
+        head = rest.astype(BF16)
+        rest = rest - head.astype(F32)
+        spread += jnp.dot(head, pick, preferred_element_type=F32)
+    row = lax.broadcasted_iota(jnp.int32, (rows, wide), 0)
+    lane = lane_of((rows, wide))
+    used = (lane < cells + rows) | (lane >= wide - rows)
+    keep = (row == lane % rows) & used
+
+    def field(index):
+        values = jnp.where(keep, spread[index * rows : (index + 1) * rows], 0.0)
+        return jnp.sum(values, axis=0, keepdims=True)
+
+    surface, below, sea = field(0), field(1), field(2)
+    wind = 0.1 * surface * surface
+
+    def renew(values, products, growth, wind, sea):
+        half = values.shape[1]
+        paired, quad_square = products[:, :half], products[:, half:]
+        return (
+            (values + 0.3 * (values * paired - quad_square) + growth * wind)
+            / (1.0 + 0.1 * values * values)
+        ) * sea
+
+    part = total // 3
+    for step in range(3):
+        span = slice(step * part, (step + 1) * part)
+        values = first_in[span, :wide].astype(F32)
+        first_in[span, wide:] = (values * values).astype(BF16)
+
+    @pl.loop(0, 3)
+    def _(step):
+        span = pl.ds(pl.multiple_of(step * part, part), part)
+        products = jnp.dot(quartet_ref[span, :], first_in[...], preferred_element_type=F32)
+        values = first_in[span, :wide].astype(F32)
+        fresh[span, :] = renew(values, products, growth_ref[span, :1], wind, sea).astype(BF16)
+
+    level = lax.broadcasted_iota(jnp.int32, (2 * levels, wide), 0)
+    forced = jnp.dot(coupler_ref[...], fresh[...], preferred_element_type=F32)
+    forced = jnp.where(level < levels, -0.3, 0.3) * forced
+
+    def beside(values):
+        first, second = values[:, :LANES], values[:, LANES:cells]
+        west, east = column_neighbours(first, second, values[:, cells:], rows)
+        lane = lane_of(first.shape)
+        west_edge = (base == 0) & (lane < rows)
+        east_edge = (base + width == grid_columns) & (lane >= LANES - rows)
+        west = (jnp.where(west_edge, 0.0, west[0]), west[1])
+        east = (east[0], jnp.where(east_edge, 0.0, east[1]))
+        sums = [
+            row_before(here, rows, False) + row_after(here, rows, False) + west[i] + east[i]
+            for i, here in enumerate((first, second))
+        ]
+        return jnp.concatenate(sums, axis=1) - 4.0 * values[:, :cells]
+
+    eight = jnp.broadcast_to(surface, (8, wide))
+    calm = surface[:, :cells] + 0.1 * beside(eight)[:1]
+    calm = calm + 0.1 * (below[:, :cells] - 2.0 * surface[:, :cells])
+    later = calm + forced[:1, :cells] - forced[levels : levels + 1, :cells]
+    later = 0.1 * later * later
+    middle = forced[:, :cells]
+    level = level[:, :cells] % levels
+    above = jnp.where(level == 0, 0.0, pltpu.roll(middle, 1, 0))
+    under = jnp.where(level == levels - 1, 0.0, pltpu.roll(middle, 2 * levels - 1, 0))
+    carried = middle + 0.1 * beside(forced) + 0.1 * (above + under - 2.0 * middle)
+
+
+    @pl.loop(0, total // 32)
+    def _(step):
+        span = pl.ds(pl.multiple_of(step * 32, 32), 32)
+        first = fresh[span, :LANES].astype(F32)
+        second = fresh[span, LANES:cells].astype(F32)
+        west, east = column_neighbours(first, second, fresh[span, cells:].astype(F32), rows)
+        cx = jnp.broadcast_to(growth_ref[span, 1:2], first.shape)
+        cy = jnp.broadcast_to(growth_ref[span, 2:3], first.shape)
+        for i, here in enumerate((first, second)):
+            moved = here - upwind(here, cx, west[i], east[i])
+            moved = moved - upwind(
+                here, cy, row_before(here, rows, True), row_after(here, rows, True)
+            )
+            moved = moved.astype(BF16)
+            second_in[span, i * LANES : (i + 1) * LANES] = moved
+            moved = moved.astype(F32)
+            second_in[span, cells + i * LANES : cells + (i + 1) * LANES] = (moved * moved).astype(
+                BF16
+            )
+
+    back = to_row_major(cells, rows, width)
+
+    @pl.loop(0, 3)
+    def _(step):
+        span = pl.ds(pl.multiple_of(step * part, part), part)
+        products = jnp.dot(quartet_ref[span, :], second_in[...], preferred_element_type=F32)
+        values = second_in[span, :cells].astype(F32)
+        done = renew(values, products, growth_ref[span, :1], later, sea[:, :cells]).astype(BF16)
+        last[span, :] = done
+        ordered[span, :] = jnp.dot(done, back, preferred_element_type=F32).astype(BF16)
+
+    forced = jnp.dot(coupler_ref[...], last[...], preferred_element_type=F32)
+    carried = carried + jnp.where(level_sign(levels, cells), -0.3, 0.3) * forced
+    carried = jnp.dot(carried.astype(BF16), back, preferred_element_type=F32)
+    half = shares.shape[1]
+    lev_parts = levels // half
+    low = lane_of((half, LANES)) < LANES // 2
+    for target in range(count):
+        cell_tile, lev_part = target // lev_parts, target % lev_parts
+        columns = slice((cell_tile // 2) * LANES, (cell_tile // 2 + 1) * LANES)
+        air = carried[lev_part * half : (lev_part + 1) * half, columns]
+        sea_part = carried[levels + lev_part * half : levels + (lev_part + 1) * half, columns]
+        if cell_tile % 2:
+            air = rolled(air, LANES // 2)
+        else:
+            sea_part = rolled(sea_part, LANES // 2)
+        shares[target] = jnp.where(low, air, sea_part).astype(BF16)
+    for slot in range(count):
+        target = lax.rem(me + slot, count)
+        span = pl.ds(pl.multiple_of(target * comps, 16), comps)
+        out_refs[slot][:comps] = ordered[span, :LANES]
+        out_refs[slot][comps : 2 * comps] = ordered[span, LANES:]
+        out_refs[slot][2 * comps :] = shares[target]
+
+
+def level_sign(levels, cells):
+    return lax.broadcasted_iota(jnp.int32, (2 * levels, cells), 0) < levels
+
+
+def finish_kernel(count, where_ref, calm_ref, *refs):
+    in_refs, refs = refs[:count], refs[count:]
+    energy_ref, air_ref, ocean_ref, pieces, wide, narrow = refs
+    comps, rows, columns = energy_ref.shape
+    levels, tile_rows, _ = air_ref.shape
+    unit = columns // count
+    me = where_ref[0]
+    part = 16
+    for slot in range(count):
+        pieces[lax.rem(me - slot + count, count)] = in_refs[slot][...]
+
+    @pl.loop(0, comps // part)
+    def _(step):
+        start = pl.multiple_of(step * part, part)
+        for tile in range(rows // count):
+            values = [
+                pieces[source, pl.ds(tile * comps + start, part), :].astype(F32)
+                for source in range(count)
+            ]
+            for row, value in enumerate(swapped_blocks(values, unit)):
+                wide[pl.ds(start * rows + tile * count + row, part, stride=rows), :] = value
+        span = pl.ds(pl.multiple_of(start * rows, part * rows), part * rows)
+        energy_ref[pl.ds(start, part)] = (
+            wide[span, :].reshape(part, rows, columns).astype(energy_ref.dtype)
+        )
+
+    for step in range(levels // part):
+        values = [
+            pieces[source, 2 * comps + step * part : 2 * comps + (step + 1) * part, :].astype(F32)
+            for source in range(count)
+        ]
+        for index, value in enumerate(swapped_blocks(values, unit)):
+            kind, row = divmod(index, tile_rows)
+            start = (kind * levels + step * part) * tile_rows + row
+            narrow[pl.ds(start, part, stride=tile_rows), :] = value
+    size = levels * tile_rows
+    air_ref[...] = calm_ref[0] + narrow[:size, :].reshape(air_ref.shape)
+    ocean_ref[...] = calm_ref[1] + narrow[size:, :].reshape(ocean_ref.shape)
+
+
+def beside_ends(block, axis, dim, width):
+    count = lax.axis_size(axis)
+    if count != 2:
+        return extended_2(block, ((axis, dim),), width, False)
+    low_end = lax.axis_index(axis) == 0
+    head = lax.slice_in_dim(block, 0, width, axis=dim)
+    tail = lax.slice_in_dim(block, block.shape[dim] - width, None, axis=dim)
+    other = lax.ppermute(jnp.where(low_end, tail, head), axis, [(0, 1), (1, 0)])
+    low = jnp.where(low_end, 0.0, other)
+    high = jnp.where(low_end, other, 0.0)
+    return jnp.concatenate([low, block, high], axis=dim)
+
+
+def twice_relaxed(state):
+    for axis, dim in (("lev", 1), ("cells", 2), ("sect", 3)):
+        state = beside_ends(state, axis, dim, 2)
+    state = relaxed(state, 1)
+    for axis, dim in (("lev", 1), ("cells", 2), ("sect", 3)):
+        place = lax.broadcasted_iota(jnp.int32, state.shape, dim)
+        index = lax.axis_index(axis)
+        outside = (index == 0) & (place == 0)
+        outside |= (index == lax.axis_size(axis) - 1) & (place == state.shape[dim] - 1)
+        state = jnp.where(outside, 0.0, state)
+    return relaxed(state, 1)
+
+
+def spread_out(pieces, axes, count):
+    received = [pieces[0]]
+    for shift in range(1, count):
+        pairs = [(index, (index + shift) % count) for index in range(count)]
+        received.append(lax.ppermute(pieces[shift], axes, pairs))
+    return received
+
+
+def by_columns(
+    spectrum, courant_x, courant_y, growth, quartet, coupler, atmosphere, ocean_state, sea_mask
+):
+    axes = ("cells", "lev")
+    count = lax.axis_size("cells") * lax.axis_size("lev")
+    sects = lax.axis_size("sect")
+    comps, rows, columns = spectrum.shape
+    total = comps * count
+    width = columns // count
+    cells = rows * width
+    levels_own, tile_rows, _ = atmosphere.shape
+    groups = max(n for n in range(1, 5) if comps % (16 * n) == 0)
+    me = lax.axis_index(axes)
+    sect = lax.axis_index("sect")
+    where = jnp.stack([me, sect * columns + me * width]).astype(jnp.int32)
+    params = pltpu.CompilerParams(vmem_limit_bytes=40 * 1024 * 1024)
+    whole = pl.BlockSpec(memory_space=VMEM)
+    scalars = pl.BlockSpec(memory_space=pltpu.SMEM)
+
+    surface = jnp.stack(
+        [atmosphere[0] - ocean_state[0], atmosphere[1] - ocean_state[1], sea_mask.astype(F32)]
+    )
+    surface = lax.all_gather(surface, ("sect",) + axes)
+    surface = surface.reshape(sects, lax.axis_size("cells"), lax.axis_size("lev"), 3, tile_rows, columns)
+    surface = surface[:, :, 0].transpose(2, 1, 3, 0, 4).reshape(3 * rows, sects * columns)
+
+    by_row, edge = pl.pallas_call(
+        edges_kernel,
+        out_shape=(
+            jax.ShapeDtypeStruct((rows, comps, columns), BF16),
+            jax.ShapeDtypeStruct((comps, LANES), BF16),
+        ),
+        in_specs=[whole],
+        out_specs=(whole, whole),
+        scratch_shapes=[VMEM((comps * rows, columns), F32)],
+        compiler_params=params,
+        name="edges",
+    )(spectrum)
+    forward = [(i, (i + 1) % sects) for i in range(sects)]
+    backward = [(target, source) for source, target in forward]
+    if sects == 2:
+        halo = lax.ppermute(edge, "sect", forward)
+    else:
+        low = lax.ppermute(edge, "sect", forward)
+        high = lax.ppermute(edge, "sect", backward)
+        halo = jnp.concatenate([low[:, : LANES // 2], high[:, LANES // 2 :]], axis=1)
+
+    column_x, column_y = courant_x[:, None], courant_y[:, None]
+    piece = jax.ShapeDtypeStruct((2 * comps + comps // groups, LANES), BF16)
+    pieces = pl.pallas_call(
+        functools.partial(advect_kernel, groups, count),
+        out_shape=(piece,) * count,
+        in_specs=[scalars] + [whole] * 5,
+        out_specs=(whole,) * count,
+        scratch_shapes=[VMEM((count,) + piece.shape, BF16), VMEM((total, cells), BF16)],
+        compiler_params=params,
+        name="advect",
+    )(where, by_row, edge, halo, column_x, column_y)
+    received = spread_out(pieces, axes, count)
+
+    factors = jnp.stack([growth, lax.all_gather(courant_x, axes, tiled=True), lax.all_gather(courant_y, axes, tiled=True)], axis=1)
+    result = jax.ShapeDtypeStruct((2 * comps + levels_own, LANES), BF16)
+    results = pl.pallas_call(
+        functools.partial(steps_kernel, groups, count),
+        out_shape=(result,) * count,
+        in_specs=[scalars] + [whole] * (4 + count),
+        out_specs=(whole,) * count,
+        scratch_shapes=[
+            VMEM((total, 6 * LANES), BF16),
+            VMEM((total, 3 * LANES), BF16),
+            VMEM((total, 4 * LANES), BF16),
+            VMEM((total, cells), BF16),
+            VMEM((total, cells), BF16),
+            VMEM((count, levels_own, LANES), BF16),
+        ],
+        compiler_params=params,
+        name="steps",
+    )(where, quartet, coupler, factors, surface, *received)
+    returned = spread_out(results, axes, count)
+
+    state = jnp.stack([atmosphere, ocean_state])
+    calm = twice_relaxed(state)
+    return pl.pallas_call(
+        functools.partial(finish_kernel, count),
+        out_shape=(
+            jax.ShapeDtypeStruct(spectrum.shape, spectrum.dtype),
+            jax.ShapeDtypeStruct(atmosphere.shape, F32),
+            jax.ShapeDtypeStruct(ocean_state.shape, F32),
+        ),
+        in_specs=[scalars] + [whole] * (1 + count),
+        out_specs=(whole,) * 3,
+        scratch_shapes=[
+            VMEM((count,) + result.shape, BF16),
+            VMEM((comps * rows, columns), F32),
+            VMEM((2 * levels_own * tile_rows, columns), F32),
+        ],
+        compiler_params=params,
+        name="finish",
+    )(where, calm, *returned)
+
+
+def on_device(spectrum, *rest):
+    atmosphere = rest[5]
+    blocks = lax.axis_size("cells") * lax.axis_size("lev")
+    comps, rows, columns = spectrum.shape
+    fits = (
+        columns == LANES
+        and blocks == 8
+        and rows * (columns // blocks) == 2 * LANES
+        and atmosphere.shape[1] * (columns // blocks) * 2 == LANES
+        and comps % 16 == 0
+        and atmosphere.shape[0] % 16 == 0
+        and NSTEP == 2
+    )
+    return (by_columns if fits else any_shape)(spectrum, *rest)
 
 
 def solution(mesh):

time: 175 us -> 140 us (0.80)
  the two profiles are of different devices: /device:TPU:0 before, /device:TPU:9 now
where the time goes in v1:
time: 140 us; the launch traced here: 139 us
  blocking collectives  45.8 us (33%)
  starting transfers between devices  24.1 us (17%)
  Pallas kernels  21.5 us (15%)
  waiting for transfers between devices  20.4 us (15%)
  local copies, waits for them, and re-layouts  13.7 us (10%)
  other arithmetic  11.7 us (8%)
  between operations  1.47 us (1%)
    all_gather x1, blocking collectives, by_columns(): surface = lax.all_gather(surface, ('sect',) + axes)  24.1 us
    unnamed x1, blocking collectives  21.7 us
    ppermute x14, waiting for transfers between devices, spread_out(): received.append(lax.ppermute(pieces[shift], axes, pairs))  17.8 us
    ppermute x14, starting transfers between devices, spread_out(): received.append(lax.ppermute(pieces[shift], axes, pairs))  14.3 us
    pallas_call x1, Pallas kernels, by_columns(): pl.pallas_call(functools.partial(steps_kernel, groups, count), out_shape=...  12.1 us
    unnamed x47, local copies, waits for them, and re-layouts  9.04 us
    ppermute x1, starting transfers between devices, extended_2(): lax.ppermute(lax.slice_in_dim(block, 0, width, axis=dim), axis, backward)  5.71 us
    pallas_call x1, Pallas kernels, by_columns(): pl.pallas_call(functools.partial(advect_kernel, groups, count), out_shape...  4.42 us
  transfers between devices with their start and end apart: 19, of which 8 were waited for; matrix products, arithmetic and copies ran while one was open for 14% of the time, Pallas kernels for 4%

profile of v1, /device:TPU:9, one launch (start us, length us, event | category | flops | bytes accessed | tf_op | source)
XLA Modules:
  0.0 138.7 jit_solution(1006528465388994684)
XLA Ops:
  2.1 1.1 copy-done.1
  3.2 1.2 edges.1
  5.2 1.2 collective-permute-start.4
  7.7 1.2 dynamic-slice
  9.4 0.9 dynamic-update-slice.1
  11.2 21.7 %all-reduce.2 = (f32[1152]{0:T(1024)S(1)}, f32[1152]{0:T(1024)S(1)}) all-reduce(f32[1152]{0:T(1024)S(1)} %dynamic-update-slice.1, f32[1152]{0:T(1024)S(1)} %dynamic-update-slice), channel_id=1, replica_groups=mesh['groups'=2,'cells'=4,'sect'=2,'lev'=2] {'cells','lev'}, use_global_device_ids=true, to_apply=%add.1 | all-reduce | flops 2304 | bytes 18432
  35.5 0.9 pad_maximum_fusion.14
  36.5 5.7 %collective-permute-start.2 = (f32[2,36,2,128]{3,2,1,0:T(2,128)S(1)}, f32[2,36,2,128]{3,2,1,0:T(2,128)S(1)}, u32[]{:S(2)}, u32[]{:S(2)}) collective-permute-start(f32[2,36,2,128]{3,2,1,0:T(2,128)S(1)} %get-tuple-element.44), channel_id=1, source_target_pairs={{4,0},{8,4},{12,8},{5,1},{9,5},{13,9},{6,2},{10,6},{14,10},{7,3},{... | collective-permute-start | bytes 221192 | tf_op jit(solution)/shard_map/ppermute | solution.py:32
  42.2 1.9 %collective-permute-start.1 = (f32[2,36,2,128]{3,2,1,0:T(2,128)S(1)}, f32[2,36,2,128]{3,2,1,0:T(2,128)S(1)}, u32[]{:S(2)}, u32[]{:S(2)}) collective-permute-start(f32[2,36,2,128]{3,2,1,0:T(2,128)S(1)} %get-tuple-element.43), channel_id=1, source_target_pairs={{0,4},{4,8},{8,12},{1,5},{5,9},{9,13},{2,6},{6,10},{10,14},{3,7},{... | collective-permute-start | bytes 221192 | tf_op jit(solution)/shard_map/ppermute | solution.py:29
  44.7 2.6 %collective-permute-done.1 = f32[2,36,2,128]{3,2,1,0:T(2,128)S(1)} collective-permute-done((f32[2,36,2,128]{3,2,1,0:T(2,128)S(1)}, f32[2,36,2,128]{3,2,1,0:T(2,128)S(1)}, u32[]{:S(2)}, u32[]{:S(2)}) %collective-permute-start.1) | collective-permute-done | bytes 73760 | tf_op jit(solution)/shard_map/ppermute | solution.py:29
  48.0 1.0 pad_maximum_fusion.13
  50.1 24.1 %all-gather = f32[48,4,128]{2,1,0:T(4,128)} all-gather(f32[3,4,128]{2,1,0:T(4,128)S(1)} %pad_maximum_fusion.17), channel_id=2, replica_groups=mesh['groups'=2,'cells'=4,'sect'=2,'lev'=2] {'sect','cells','lev'}, dimensions={0}, use_global_device_ids=true | all-gather | bytes 104448 | tf_op jit(solution)/shard_map/all_gather | solution.py:518
  74.2 1.0 copy.22.growth_ref
  77.4 1.4 %copy.21.cy_ref = f32[144,1]{1,0:T(8,128)} copy(f32[144,1]{0,1:T(1,128)} %bitcast.32) | data formatting | bytes 1152 | tf_op jit(solution)/shard_map/broadcast_in_dim | solution.py:543
  78.8 1.1 copy-done.3
  79.9 0.9 copy-done.5
  81.7 4.4 %advect.1 = (bf16[336,128]{1,0:T(8,128)(2,1)S(1)}, bf16[336,128]{1,0:T(8,128)(2,1)S(1)}, bf16[336,128]{1,0:T(8,128)(2,1)S(1)}, bf16[336,128]{1,0:T(8,128)(2,1)S(...) custom-call(s32[2]{0:T(128)S(1)} %pad_add_fusion.where_ref, ...), custom_call_target="tpu_custom_call" | custom-call | tf_op jit(solution)/shard_map/advect/pallas_call | solution.py:545
  86.9 4.2 %collective-permute-start.7 = (bf16[336,128]{1,0:T(8,128)(2,1)S(1)}, bf16[336,128]{1,0:T(8,128)(2,1)S(1)}, u32[]{:S(2)}, u32[]{:S(2)}) collective-permute-start(bf16[336,128]{1,0:T(8,128)(2,1)S(1)} %get-tuple-element.26), channel_id=1, source_target_pairs={{0,5},{1,8},{4,9},{5,12},{8,13},{9,0},{12,1},{13,4},{2,7},{3,10},{... | collective-permute-start | bytes 258056 | tf_op jit(solution)/shard_map/ppermute | solution.py:492
  91.1 1.4 %collective-permute-start.9 = (bf16[336,128]{1,0:T(8,128)(2,1)S(1)}, bf16[336,128]{1,0:T(8,128)(2,1)S(1)}, u32[]{:S(2)}, u32[]{:S(2)}) collective-permute-start(bf16[336,128]{1,0:T(8,128)(2,1)S(1)} %get-tuple-element.28), channel_id=1, source_target_pairs={{0,9},{1,12},{4,13},{5,0},{8,1},{9,4},{12,5},{13,8},{2,11},{3,14},... | collective-permute-start | bytes 258056 | tf_op jit(solution)/shard_map/ppermute | solution.py:492
  92.5 1.0 broadcast_select_fusion.1
  93.5 2.4 %collective-permute-start.10 = (bf16[336,128]{1,0:T(8,128)(2,1)S(1)}, bf16[336,128]{1,0:T(8,128)(2,1)S(1)}, u32[]{:S(2)}, u32[]{:S(2)}) collective-permute-start(bf16[336,128]{1,0:T(8,128)(2,1)S(1)} %get-tuple-element.29), channel_id=1, source_target_pairs={{0,12},{1,13},{4,0},{5,1},{8,4},{9,5},{12,8},{13,9},{2,14},{3,15},... | collective-permute-start | bytes 258056 | tf_op jit(solution)/shard_map/ppermute | solution.py:492
  96.0 1.7 %pad_maximum_fusion = f32[2,36,8,132]{3,2,1,0:T(8,128)S(1)} fusion(f32[2,36,8,2]{3,2,1,0:T(8,128)S(1)} %get-tuple-element.42, f32[2,36,2,128]{3,2,1,0:T(2,128)} %copy-done.10, f32[2,2,4,128]{3,2,1,0:T(4,128)} %copy-done.14, f32[1,32,4,128]{3,2,1,0:T(4,128)} %bitcast.22, f32[1,32,4,128]{3,2,1,0:T(4,128)} %bitcast.27, f32[2,2,4,128]{3,2,1,0:T(4,128)S(1)} %get-tuple-element.47, ...), kind=kLoop, calls=%fused_computation | loop fusion | flops 532224 | bytes 608256 | tf_op jit(solution)/shard_map/concatenate | solution.py:472
  97.7 3.0 %collective-permute-done.7.refs_3_ = bf16[336,128]{1,0:T(8,128)(2,1)S(1)} collective-permute-done((bf16[336,128]{1,0:T(8,128)(2,1)S(1)}, bf16[336,128]{1,0:T(8,128)(2,1)S(1)}, u32[]{:S(2)}, u32[]{:S(2)}) %collective-permute-start.7) | collective-permute-done | bytes 86048 | tf_op jit(solution)/shard_map/ppermute | solution.py:492
  100.7 1.8 %collective-permute-done.8.refs_4_ = bf16[336,128]{1,0:T(8,128)(2,1)S(1)} collective-permute-done((bf16[336,128]{1,0:T(8,128)(2,1)S(1)}, bf16[336,128]{1,0:T(8,128)(2,1)S(1)}, u32[]{:S(2)}, u32[]{:S(2)}) %collective-permute-start.8) | collective-permute-done | bytes 86048 | tf_op jit(solution)/shard_map/ppermute | solution.py:492
  102.5 3.6 %collective-permute-done.10.refs_6_ = bf16[336,128]{1,0:T(8,128)(2,1)S(1)} collective-permute-done((bf16[336,128]{1,0:T(8,128)(2,1)S(1)}, bf16[336,128]{1,0:T(8,128)(2,1)S(1)}, u32[]{:S(2)}, u32[]{:S(2)}) %collective-permute-start.10) | collective-permute-done | bytes 86048 | tf_op jit(solution)/shard_map/ppermute | solution.py:492
  106.2 12.1 %steps.1 = (bf16[320,128]{1,0:T(8,128)(2,1)S(1)}, bf16[320,128]{1,0:T(8,128)(2,1)S(1)}, bf16[320,128]{1,0:T(8,128)(2,1)S(1)}, bf16[320,128]{1,0:T(8,128)(2,1)S(1...) custom-call(s32[2]{0:T(128)S(1)} %pad_add_fusion.where_ref, ...), custom_call_target="tpu_custom_call" | custom-call | tf_op jit(solution)/shard_map/steps/pallas_call | solution.py:558
  118.5 1.3 fusion.5
  120.4 2.2 %collective-permute-start.15 = (bf16[320,128]{1,0:T(8,128)(2,1)S(1)}, bf16[320,128]{1,0:T(8,128)(2,1)S(1)}, u32[]{:S(2)}, u32[]{:S(2)}) collective-permute-start(bf16[320,128]{1,0:T(8,128)(2,1)S(1)} %get-tuple-element.35), channel_id=1, source_target_pairs={{0,8},{1,9},{4,12},{5,13},{8,0},{9,1},{12,4},{13,5},{2,10},{3,11},... | collective-permute-start | bytes 245768 | tf_op jit(solution)/shard_map/ppermute | solution.py:492
  122.5 1.6 %collective-permute-start.16 = (bf16[320,128]{1,0:T(8,128)(2,1)S(1)}, bf16[320,128]{1,0:T(8,128)(2,1)S(1)}, u32[]{:S(2)}, u32[]{:S(2)}) collective-permute-start(bf16[320,128]{1,0:T(8,128)(2,1)S(1)} %get-tuple-element.36), channel_id=1, source_target_pairs={{0,9},{1,12},{4,13},{5,0},{8,1},{9,4},{12,5},{13,8},{2,11},{3,14},... | collective-permute-start | bytes 245768 | tf_op jit(solution)/shard_map/ppermute | solution.py:492
  125.6 5.9 %collective-permute-done.15.refs_4_ = bf16[320,128]{1,0:T(8,128)(2,1)S(1)} collective-permute-done((bf16[320,128]{1,0:T(8,128)(2,1)S(1)}, bf16[320,128]{1,0:T(8,128)(2,1)S(1)}, u32[]{:S(2)}, u32[]{:S(2)}) %collective-permute-start.15) | collective-permute-done | bytes 81952 | tf_op jit(solution)/shard_map/ppermute | solution.py:492
  131.5 3.3 %collective-permute-done.17.refs_6_ = bf16[320,128]{1,0:T(8,128)(2,1)S(1)} collective-permute-done((bf16[320,128]{1,0:T(8,128)(2,1)S(1)}, bf16[320,128]{1,0:T(8,128)(2,1)S(1)}, u32[]{:S(2)}, u32[]{:S(2)}) %collective-permute-start.17) | collective-permute-done | bytes 81952 | tf_op jit(solution)/shard_map/ppermute | solution.py:492
  134.9 3.8 %finish.1 = (bf16[144,16,128]{2,1,0:T(8,128)(2,1)}, f32[32,4,128]{2,1,0:T(4,128)}, f32[32,4,128]{2,1,0:T(4,128)}) custom-call(s32[2]{0:T(128)S(1)} %pad_add_fusion.where_ref, f32[2,32,4,128]{3,2,1,0:T(4,128)S(1)} %fusion.13.calm_ref, bf16[320,128]{1,0:T(8,128)(2,1)S(1)} %get-tuple-element.31.refs_0_, bf16[320,128]{1,0:T(8,128)(2,1)S(1)} %collective-permute-done.12.refs_1_, ...), custom_call_target="tpu_custom_call" | custom-call | tf_op jit(solution)/shard_map/finish/pallas_call | solution.py:578
  (84 shorter events, 15.6 us)
Async XLA Ops:
  0.6 76.0 %copy-start.16 = (f32[144]{0:T(256)S(1)}, f32[144]{0:T(256)}, u32[]{:S(2)}) copy-start(f32[144]{0:T(256)} %param.10) | copy-start | bytes 1732
  1.4 34.1 %collective-permute-start = (f32[2,2,4,128]{3,2,1,0:T(4,128)S(1)}, f32[2,2,4,128]{3,2,1,0:T(4,128)S(1)}, u32[]{:S(2)}, u32[]{:S(2)}) collective-permute-start(f32[2,2,4,128]{3,2,1,0:T(4,128)S(1)} %fusion.17), channel_id=1, source_target_pairs={{0,1},{1,0},{2,3},{3,2},{4,5},{5,4},{6,7},{7,6},{8,9},{9,8},{10,11... | collective-permute-start | bytes 24584 | tf_op jit(solution)/shard_map/ppermute | solution.py:469
  5.2 73.6 %collective-permute-start.4 = (bf16[144,128]{1,0:T(8,128)(2,1)}, bf16[144,128]{1,0:T(8,128)(2,1)}, u32[]{:S(2)}, u32[]{:S(2)}) collective-permute-start(bf16[144,128]{1,0:T(8,128)(2,1)} %get-tuple-element.22.edge_ref), channel_id=1, source_target_pairs={{0,2},{2,0},{1,3},{3,1},{4,6},{6,4},{5,7},{7,5},{8,10},{10,8},{9,1... | collective-permute-start | bytes 110600 | tf_op jit(solution)/shard_map/ppermute | solution.py:537
  35.5 11.8 %copy-start.14 = (f32[2,2,4,128]{3,2,1,0:T(4,128)}, f32[2,2,4,128]{3,2,1,0:T(4,128)S(1)}, u32[]{:S(2)}) copy-start(f32[2,2,4,128]{3,2,1,0:T(4,128)S(1)} %get-tuple-element.48) | copy-start | bytes 24580
  36.5 8.2 %collective-permute-start.2 = (f32[2,36,2,128]{3,2,1,0:T(2,128)S(1)}, f32[2,36,2,128]{3,2,1,0:T(2,128)S(1)}, u32[]{:S(2)}, u32[]{:S(2)}) collective-permute-start(f32[2,36,2,128]{3,2,1,0:T(2,128)S(1)} %get-tuple-element.44), channel_id=1, source_target_pairs={{4,0},{8,4},{12,8},{5,1},{9,5},{13,9},{6,2},{10,6},{14,10},{7,3},{... | collective-permute-start | bytes 221192 | tf_op jit(solution)/shard_map/ppermute | solution.py:32
  42.2 5.1 %collective-permute-start.1 = (f32[2,36,2,128]{3,2,1,0:T(2,128)S(1)}, f32[2,36,2,128]{3,2,1,0:T(2,128)S(1)}, u32[]{:S(2)}, u32[]{:S(2)}) collective-permute-start(f32[2,36,2,128]{3,2,1,0:T(2,128)S(1)} %get-tuple-element.43), channel_id=1, source_target_pairs={{0,4},{4,8},{8,12},{1,5},{5,9},{9,13},{2,6},{6,10},{10,14},{3,7},{... | collective-permute-start | bytes 221192 | tf_op jit(solution)/shard_map/ppermute | solution.py:29
  48.0 58.2 %copy-start.4 = (bf16[128,1152]{1,0:T(8,128)(2,1)S(1)}, bf16[128,1152]{1,0:T(8,128)(2,1)}, u32[]{:S(2)}) copy-start(bf16[128,1152]{1,0:T(8,128)(2,1)} %coupler_ref.1) | copy-start | bytes 884740
  49.0 57.2 %copy-start = (bf16[1152,1152]{1,0:T(8,128)(2,1)S(1)}, bf16[1152,1152]{1,0:T(8,128)(2,1)}, u32[]{:S(2)}) copy-start(bf16[1152,1152]{1,0:T(8,128)(2,1)} %quartet_ref.1) | copy-start | bytes 7962628
  49.9 41.2 %collective-permute-start.3 = (f32[2,36,8,2]{3,2,1,0:T(8,128)}, f32[2,36,8,2]{3,2,1,0:T(8,128)}, u32[]{:S(2)}, u32[]{:S(2)}) collective-permute-start(f32[2,36,8,2]{3,2,1,0:T(8,128)} %slice_select_fusion), channel_id=1, source_target_pairs={{0,2},{2,0},{1,3},{3,1},{4,6},{6,4},{5,7},{7,5},{8,10},{10,8},{9,1... | collective-permute-start | bytes 13832 | tf_op jit(solution)/shard_map/ppermute | solution.py:469
  81.7 24.5 %copy-start.7 = (f32[6,8,2,128]{3,1,2,0:T(8,128)S(1)}, f32[6,8,2,128]{3,1,2,0:T(8,128)}, u32[]{:S(2)}) copy-start(f32[6,8,2,128]{3,1,2,0:T(8,128)} %copy.26) | copy-start | bytes 147460
  86.1 7.4 %collective-permute-start.5 = (bf16[336,128]{1,0:T(8,128)(2,1)S(1)}, bf16[336,128]{1,0:T(8,128)(2,1)S(1)}, u32[]{:S(2)}, u32[]{:S(2)}) collective-permute-start(bf16[336,128]{1,0:T(8,128)(2,1)S(1)} %get-tuple-element.24), channel_id=1, source_target_pairs={{0,1},{1,4},{4,5},{5,8},{8,9},{9,12},{12,13},{13,0},{2,3},{3,6},{6... | collective-permute-start | bytes 258056 | tf_op jit(solution)/shard_map/ppermute | solution.py:492
  86.2 9.7 %collective-permute-start.6 = (bf16[336,128]{1,0:T(8,128)(2,1)S(1)}, bf16[336,128]{1,0:T(8,128)(2,1)S(1)}, u32[]{:S(2)}, u32[]{:S(2)}) collective-permute-start(bf16[336,128]{1,0:T(8,128)(2,1)S(1)} %get-tuple-element.25), channel_id=1, source_target_pairs={{0,4},{1,5},{4,8},{5,9},{8,12},{9,13},{12,0},{13,1},{2,6},{3,7},{6... | collective-permute-start | bytes 258056 | tf_op jit(solution)/shard_map/ppermute | solution.py:492
  86.9 13.8 %collective-permute-start.7 = (bf16[336,128]{1,0:T(8,128)(2,1)S(1)}, bf16[336,128]{1,0:T(8,128)(2,1)S(1)}, u32[]{:S(2)}, u32[]{:S(2)}) collective-permute-start(bf16[336,128]{1,0:T(8,128)(2,1)S(1)} %get-tuple-element.26), channel_id=1, source_target_pairs={{0,5},{1,8},{4,9},{5,12},{8,13},{9,0},{12,1},{13,4},{2,7},{3,10},{... | collective-permute-start | bytes 258056 | tf_op jit(solution)/shard_map/ppermute | solution.py:492
  91.1 11.4 %collective-permute-start.8 = (bf16[336,128]{1,0:T(8,128)(2,1)S(1)}, bf16[336,128]{1,0:T(8,128)(2,1)S(1)}, u32[]{:S(2)}, u32[]{:S(2)}) collective-permute-start(bf16[336,128]{1,0:T(8,128)(2,1)S(1)} %get-tuple-element.27), channel_id=1, source_target_pairs={{0,8},{1,9},{4,12},{5,13},{8,0},{9,1},{12,4},{13,5},{2,10},{3,11},... | collective-permute-start | bytes 258056 | tf_op jit(solution)/shard_map/ppermute | solution.py:492
  91.1 11.4 %collective-permute-start.9 = (bf16[336,128]{1,0:T(8,128)(2,1)S(1)}, bf16[336,128]{1,0:T(8,128)(2,1)S(1)}, u32[]{:S(2)}, u32[]{:S(2)}) collective-permute-start(bf16[336,128]{1,0:T(8,128)(2,1)S(1)} %get-tuple-element.28), channel_id=1, source_target_pairs={{0,9},{1,12},{4,13},{5,0},{8,1},{9,4},{12,5},{13,8},{2,11},{3,14},... | collective-permute-start | bytes 258056 | tf_op jit(solution)/shard_map/ppermute | solution.py:492
  93.5 12.6 %collective-permute-start.10 = (bf16[336,128]{1,0:T(8,128)(2,1)S(1)}, bf16[336,128]{1,0:T(8,128)(2,1)S(1)}, u32[]{:S(2)}, u32[]{:S(2)}) collective-permute-start(bf16[336,128]{1,0:T(8,128)(2,1)S(1)} %get-tuple-element.29), channel_id=1, source_target_pairs={{0,12},{1,13},{4,0},{5,1},{8,4},{9,5},{12,8},{13,9},{2,14},{3,15},... | collective-permute-start | bytes 258056 | tf_op jit(solution)/shard_map/ppermute | solution.py:492
  95.9 10.3 %collective-permute-start.11 = (bf16[336,128]{1,0:T(8,128)(2,1)S(1)}, bf16[336,128]{1,0:T(8,128)(2,1)S(1)}, u32[]{:S(2)}, u32[]{:S(2)}) collective-permute-start(bf16[336,128]{1,0:T(8,128)(2,1)S(1)} %get-tuple-element.30), channel_id=1, source_target_pairs={{0,13},{1,0},{4,1},{5,4},{8,5},{9,8},{12,9},{13,12},{2,15},{3,2},{... | collective-permute-start | bytes 258056 | tf_op jit(solution)/shard_map/ppermute | solution.py:492
  95.9 22.6 %copy-start.8 = (f32[32,4,128]{2,1,0:T(4,128)S(1)}, f32[32,4,128]{2,1,0:T(4,128)}, u32[]{:S(2)}) copy-start(f32[32,4,128]{2,1,0:T(4,128)} %param.16) | copy-start | bytes 196612
  95.9 22.6 %copy-start.9 = (f32[32,4,128]{2,1,0:T(4,128)S(1)}, f32[32,4,128]{2,1,0:T(4,128)}, u32[]{:S(2)}) copy-start(f32[32,4,128]{2,1,0:T(4,128)} %param.15) | copy-start | bytes 196612
  95.9 22.6 %copy-start.11 = (f32[2,36,2,128]{3,2,1,0:T(2,128)S(1)}, f32[2,36,2,128]{3,2,1,0:T(2,128)}, u32[]{:S(2)}) copy-start(f32[2,36,2,128]{3,2,1,0:T(2,128)} %copy-done.10) | copy-start | bytes 221188
  95.9 22.6 %copy-start.13 = (f32[2,36,2,128]{3,2,1,0:T(2,128)S(1)}, f32[2,36,2,128]{3,2,1,0:T(2,128)}, u32[]{:S(2)}) copy-start(f32[2,36,2,128]{3,2,1,0:T(2,128)} %copy-done.12) | copy-start | bytes 221188
  95.9 22.6 %copy-start.15 = (f32[2,2,4,128]{3,2,1,0:T(4,128)S(1)}, f32[2,2,4,128]{3,2,1,0:T(4,128)}, u32[]{:S(2)}) copy-start(f32[2,2,4,128]{3,2,1,0:T(4,128)} %copy-done.14) | copy-start | bytes 24580
  96.0 22.6 %copy-start.17 = (pred[34]{0:T(512)(128)(4,1)S(1)}, pred[34]{0:T(512)(128)(4,1)}, u32[]{:S(2)}) copy-start(pred[34]{0:T(512)(128)(4,1)} %and_or_fusion) | copy-start | bytes 106
  96.0 22.6 %copy-start.18 = (pred[6]{0:T(512)(128)(4,1)S(1)}, pred[6]{0:T(512)(128)(4,1)}, u32[]{:S(2)}) copy-start(pred[6]{0:T(512)(128)(4,1)} %and_or_fusion.1) | copy-start | bytes 22
  96.0 22.6 %copy-start.19 = (pred[130]{0:T(512)(128)(4,1)S(1)}, pred[130]{0:T(512)(128)(4,1)}, u32[]{:S(2)}) copy-start(pred[130]{0:T(512)(128)(4,1)} %and_or_fusion.2) | copy-start | bytes 394
  118.3 5.8 %collective-permute-start.12 = (bf16[320,128]{1,0:T(8,128)(2,1)S(1)}, bf16[320,128]{1,0:T(8,128)(2,1)S(1)}, u32[]{:S(2)}, u32[]{:S(2)}) collective-permute-start(bf16[320,128]{1,0:T(8,128)(2,1)S(1)} %get-tuple-element.32), channel_id=1, source_target_pairs={{0,1},{1,4},{4,5},{5,8},{8,9},{9,12},{12,13},{13,0},{2,3},{3,6},{6... | collective-permute-start | bytes 245768 | tf_op jit(solution)/shard_map/ppermute | solution.py:492
  118.4 6.5 %collective-permute-start.13 = (bf16[320,128]{1,0:T(8,128)(2,1)S(1)}, bf16[320,128]{1,0:T(8,128)(2,1)S(1)}, u32[]{:S(2)}, u32[]{:S(2)}) collective-permute-start(bf16[320,128]{1,0:T(8,128)(2,1)S(1)} %get-tuple-element.33), channel_id=1, source_target_pairs={{0,4},{1,5},{4,8},{5,9},{8,12},{9,13},{12,0},{13,1},{2,6},{3,7},{6... | collective-permute-start | bytes 245768 | tf_op jit(solution)/shard_map/ppermute | solution.py:492
  119.8 5.8 %collective-permute-start.14 = (bf16[320,128]{1,0:T(8,128)(2,1)S(1)}, bf16[320,128]{1,0:T(8,128)(2,1)S(1)}, u32[]{:S(2)}, u32[]{:S(2)}) collective-permute-start(bf16[320,128]{1,0:T(8,128)(2,1)S(1)} %get-tuple-element.34), channel_id=1, source_target_pairs={{0,5},{1,8},{4,9},{5,12},{8,13},{9,0},{12,1},{13,4},{2,7},{3,10},{... | collective-permute-start | bytes 245768 | tf_op jit(solution)/shard_map/ppermute | solution.py:492
  120.4 11.2 %collective-permute-start.15 = (bf16[320,128]{1,0:T(8,128)(2,1)S(1)}, bf16[320,128]{1,0:T(8,128)(2,1)S(1)}, u32[]{:S(2)}, u32[]{:S(2)}) collective-permute-start(bf16[320,128]{1,0:T(8,128)(2,1)S(1)} %get-tuple-element.35), channel_id=1, source_target_pairs={{0,8},{1,9},{4,12},{5,13},{8,0},{9,1},{12,4},{13,5},{2,10},{3,11},... | collective-permute-start | bytes 245768 | tf_op jit(solution)/shard_map/ppermute | solution.py:492
  122.5 9.0 %collective-permute-start.16 = (bf16[320,128]{1,0:T(8,128)(2,1)S(1)}, bf16[320,128]{1,0:T(8,128)(2,1)S(1)}, u32[]{:S(2)}, u32[]{:S(2)}) collective-permute-start(bf16[320,128]{1,0:T(8,128)(2,1)S(1)} %get-tuple-element.36), channel_id=1, source_target_pairs={{0,9},{1,12},{4,13},{5,0},{8,1},{9,4},{12,5},{13,8},{2,11},{3,14},... | collective-permute-start | bytes 245768 | tf_op jit(solution)/shard_map/ppermute | solution.py:492
  124.1 10.8 %collective-permute-start.17 = (bf16[320,128]{1,0:T(8,128)(2,1)S(1)}, bf16[320,128]{1,0:T(8,128)(2,1)S(1)}, u32[]{:S(2)}, u32[]{:S(2)}) collective-permute-start(bf16[320,128]{1,0:T(8,128)(2,1)S(1)} %get-tuple-element.37), channel_id=1, source_target_pairs={{0,12},{1,13},{4,0},{5,1},{8,4},{9,5},{12,8},{13,9},{2,14},{3,15},... | collective-permute-start | bytes 245768 | tf_op jit(solution)/shard_map/ppermute | solution.py:492
  124.8 10.1 %collective-permute-start.18 = (bf16[320,128]{1,0:T(8,128)(2,1)S(1)}, bf16[320,128]{1,0:T(8,128)(2,1)S(1)}, u32[]{:S(2)}, u32[]{:S(2)}) collective-permute-start(bf16[320,128]{1,0:T(8,128)(2,1)S(1)} %get-tuple-element.38), channel_id=1, source_target_pairs={{0,13},{1,0},{4,1},{5,4},{8,5},{9,8},{12,9},{13,12},{2,15},{3,2},{... | collective-permute-start | bytes 245768 | tf_op jit(solution)/shard_map/ppermute | solution.py:492
  (7 other events, 8.0 us)

commit v2 on v1

--- a/solution.py
+++ b/solution.py
@@ -177,8 +177,18 @@
     return ((target % width) * rows + target // width == source).astype(BF16)
 
 
-def edges_kernel(x_ref, by_row_ref, edge_ref, wide):
+def split(values):
+    head = values.astype(BF16).astype(F32)
+    return head, values - head
+
+
+def column_of(row, lanes):
+    return jnp.transpose(jnp.broadcast_to(row, (lanes, row.shape[1])))
+
+
+def edges_kernel(x_ref, air_ref, ocean_ref, sea_ref, by_row_ref, edge_ref, below_ref, wide):
     comps, rows, columns = x_ref.shape
+    tile_rows = sea_ref.shape[0]
     wide[...] = x_ref[...].astype(F32).reshape(comps * rows, columns)
     column = lax.broadcasted_iota(jnp.int32, (columns, LANES), 0)
     lane = lax.broadcasted_iota(jnp.int32, (columns, LANES), 1)
@@ -190,21 +200,32 @@
         by_row_ref[row] = values
         pick = ((wanted == column) & (lane % rows == row)).astype(BF16)
         total += jnp.dot(values, pick, preferred_element_type=F32)
-    edge_ref[...] = total.astype(BF16)
-
-
-def advect_kernel(groups, count, where_ref, by_row_ref, edge_ref, halo_ref, cx_ref, cy_ref, *refs):
-    out_refs, (packed, cell_major) = refs[:count], refs[count:]
+    edge_ref[:comps] = total.astype(BF16)
+    owner = jnp.where(lax.axis_index("lev") == 0, 1.0, 0.0)
+    head, tail = split((air_ref[0] - ocean_ref[0]) * owner)
+    sea = sea_ref[...].astype(F32) * owner
+    none = jnp.zeros_like(sea)
+    edge_ref[comps:] = jnp.concatenate([head, tail, sea, none], axis=0).astype(BF16)
+    head, tail = split((air_ref[1] - ocean_ref[1]) * owner)
+    below_ref[...] = jnp.concatenate([head, tail, none, none], axis=0).astype(BF16)
+
+
+def advect_kernel(
+    groups, count, by_row_ref, edge_ref, below_ref, halo_ref, courant_x_ref, courant_y_ref, *refs
+):
+    out_refs, (packed, cell_major, cx_ref, cy_ref) = refs[:count], refs[count:]
     rows, comps, columns = by_row_ref.shape
     width = columns // count
     part = 16
+    cx_ref[...] = column_of(courant_x_ref[...], LANES)
+    cy_ref[...] = column_of(courant_y_ref[...], LANES)
 
     @pl.loop(0, comps // part)
     def _(step):
         start = pl.multiple_of(step * part, part)
         values = [by_row_ref[row, pl.ds(start, part), :].astype(F32) for row in range(rows)]
-        cx = jnp.broadcast_to(cx_ref[pl.ds(start, part), :], (part, columns))
-        cy = jnp.broadcast_to(cy_ref[pl.ds(start, part), :], (part, columns))
+        cx = cx_ref[pl.ds(start, part), :]
+        cy = cy_ref[pl.ds(start, part), :]
         moved = []
         for row in range(rows):
             here = values[row]
@@ -222,11 +243,11 @@
     change = to_column_major(rows * width, rows, width)
     lane = lane_of((comps, LANES))
     block = lane // rows
-    halo = halo_ref[...].astype(F32)
-    edge = edge_ref[...].astype(F32)
+    halo = halo_ref[:comps].astype(F32)
+    edge = edge_ref[:comps].astype(F32)
     near = jnp.where((block < 2) | (block >= 6), halo, edge)
-    cx = jnp.broadcast_to(cx_ref[...], (comps, LANES))
-    cy = jnp.broadcast_to(cy_ref[...], (comps, LANES))
+    cx = cx_ref[...]
+    cy = cy_ref[...]
     near = (
         near
         - upwind(near, cx, rolled(near, rows), rolled(near, -rows))
@@ -243,7 +264,55 @@
     tiles[0][0] = jnp.where(block == 0, rolled(near, -2 * rows), tiles[0][0])
     tiles[-1][1] = jnp.where(block == 7, rolled(near, 2 * rows), tiles[-1][1])
     size = comps // groups
-    me = where_ref[0]
+    me = lax.axis_index(("cells", "lev"))
+
+    own = lane_of((size, LANES))
+    riders = jnp.zeros((size, LANES), F32)
+    for group in range(groups):
+        span = slice(group * size, (group + 1) * size)
+        for index, term in enumerate(split(cx[span]) + split(cy[span])):
+            riders = jnp.where(own == 5 * rows + 4 * group + index, term, riders)
+
+    tile_rows = 4
+    cells = rows * width
+    values = jnp.concatenate([edge_ref[comps:], below_ref[...]], axis=0)
+    spot = lax.broadcasted_iota(jnp.int32, (columns, count * cells), 0)
+    lanes = lax.broadcasted_iota(jnp.int32, (columns, count * cells), 1)
+    repeat = (lanes // rows == spot).astype(BF16)
+    inland = jnp.dot(values, repeat, preferred_element_type=F32)
+    spot = lax.broadcasted_iota(jnp.int32, (columns, LANES), 0)
+    lanes = lax.broadcasted_iota(jnp.int32, (columns, LANES), 1)
+    repeat = ((lanes < rows) & (spot == columns - 1)) | ((lanes >= LANES - rows) & (spot == 0))
+    coast = jnp.dot(halo_ref[comps:], repeat.astype(BF16), preferred_element_type=F32)
+    coast = jnp.concatenate([coast, jnp.zeros_like(coast)], axis=0)
+    first_row = lax.axis_index("cells") * tile_rows
+
+    def gathered(values):
+        place = lax.broadcasted_iota(jnp.int32, values.shape, 0)
+        lanes = lane_of(values.shape)
+        kept = jnp.where(lanes % rows == first_row + place % tile_rows, values, 0.0).astype(BF16)
+        target = lax.broadcasted_iota(jnp.int32, (8, values.shape[0]), 0)
+        source = lax.broadcasted_iota(jnp.int32, (8, values.shape[0]), 1) // tile_rows
+        source = jnp.where(source < 3, source, jnp.where(source < 4, 7, source - 1))
+        adds = (target == jnp.where(source < 5, source, 7)).astype(BF16)
+        return jnp.dot(adds, kept, preferred_element_type=F32)
+
+    inland, coast = gathered(inland), gathered(coast)
+    place = lax.broadcasted_iota(jnp.int32, (8, LANES), 0)
+    for target in range(count):
+        tile = 2 * target
+        winds = [inland[:, (tile + i) * LANES : (tile + i + 1) * LANES] for i in range(2)]
+        before = coast
+        if target:
+            before = rolled(inland[:, (tile - 1) * LANES : tile * LANES], rows)
+        after = coast
+        if target < count - 1:
+            after = rolled(inland[:, (tile + 2) * LANES : (tile + 3) * LANES], -rows)
+        ends = jnp.where(lane_of(before.shape) < rows, before, after)
+        winds[0] = jnp.where(place < 5, winds[0], pltpu.roll(ends, 5, 0))
+        slot = lax.rem(target - me + count, count)
+        packed[slot, 2 * comps + size :, :] = jnp.concatenate(winds, axis=0).astype(BF16)
+
     for target in range(count):
         west = rolled(tiles[target - 1][1], rows) if target else rolled(near, -rows)
         east = rolled(tiles[target + 1][0], -rows) if target < count - 1 else rolled(near, rows)
@@ -253,69 +322,64 @@
             other = rolled(outer[group * size : (group + 1) * size], 2 * group * rows)
             own = lane_of(other.shape) // rows
             shared = jnp.where((own == 2 * group) | (own == 2 * group - 1), other, shared)
+        own = lane_of(shared.shape) // rows
+        shared = jnp.where((own == 5) | (own == 6), riders, shared)
         slot = lax.rem(target - me + count, count)
         packed[slot, :comps, :] = tiles[target][0].astype(BF16)
         packed[slot, comps : 2 * comps, :] = tiles[target][1].astype(BF16)
-        packed[slot, 2 * comps :, :] = shared.astype(BF16)
+        packed[slot, 2 * comps : 2 * comps + size, :] = shared.astype(BF16)
     for slot in range(count):
         out_refs[slot][...] = packed[slot]
 
 
-def steps_kernel(groups, count, where_ref, quartet_ref, coupler_ref, growth_ref, surface_ref, *refs):
+def steps_kernel(groups, count, rows, quartet_ref, coupler_ref, growth_ref, *refs):
     in_refs, refs = refs[:count], refs[count:]
-    out_refs, (first_in, fresh, second_in, last, ordered, shares) = refs[:count], refs[count:]
+    out_refs, refs = refs[:count], refs[count:]
+    first_in, fresh, second_in, last, ordered, shares, factors = refs
     total = quartet_ref.shape[0]
     comps = total // count
     size = comps // groups
-    rows = surface_ref.shape[0] // 3
-    grid_columns = surface_ref.shape[1]
     cells = 2 * LANES
     wide = 3 * LANES
     width = cells // rows
     levels = coupler_ref.shape[0] // 2
-    me = where_ref[0]
-    base = where_ref[1]
-
+    me = lax.axis_index(("cells", "lev"))
+    west_end = (me == 0) & (lax.axis_index("sect") == 0)
+    east_end = (me == count - 1) & (lax.axis_index("sect") == lax.axis_size("sect") - 1)
+    factors[:, 8:16] = column_of(0.1 * growth_ref[...], 8)
+
+    winds = jnp.zeros((16, LANES), F32)
     for slot in range(count):
         source = lax.rem(me - slot + count, count)
         start = pl.multiple_of(source * comps, 16)
         first_in[pl.ds(start, comps), :LANES] = in_refs[slot][:comps]
         first_in[pl.ds(start, comps), LANES:cells] = in_refs[slot][comps : 2 * comps]
-        shared = in_refs[slot][2 * comps :].astype(F32)
+        shared = in_refs[slot][2 * comps : 2 * comps + size].astype(F32)
+        courant = shared + rolled(shared, -1)
         for group in range(groups):
-            first_in[pl.ds(start + group * size, size), cells:wide] = rolled(
-                shared, -2 * group * rows
-            ).astype(BF16)
-
-    lane = lane_of((grid_columns, wide))
-    offset = jnp.where(lane < cells, lane // rows, jnp.where(lane < cells + rows, -1, width))
-    wanted = lax.rem(base + offset + grid_columns, grid_columns)
-    pick = (lax.broadcasted_iota(jnp.int32, (grid_columns, wide), 0) == wanted).astype(BF16)
-    rest = surface_ref[...]
-    spread = jnp.zeros((3 * rows, wide), F32)
-    for _ in range(3):
-        head = rest.astype(BF16)
-        rest = rest - head.astype(F32)
-        spread += jnp.dot(head, pick, preferred_element_type=F32)
-    row = lax.broadcasted_iota(jnp.int32, (rows, wide), 0)
-    lane = lane_of((rows, wide))
-    used = (lane < cells + rows) | (lane >= wide - rows)
-    keep = (row == lane % rows) & used
-
-    def field(index):
-        values = jnp.where(keep, spread[index * rows : (index + 1) * rows], 0.0)
-        return jnp.sum(values, axis=0, keepdims=True)
-
-    surface, below, sea = field(0), field(1), field(2)
-    wind = 0.1 * surface * surface
+            span = pl.ds(pl.multiple_of(start + group * size, 16), size)
+            first_in[span, cells:wide] = rolled(shared, -2 * group * rows).astype(BF16)
+            factors[span, :8] = rolled(courant, -5 * rows - 4 * group)[:, :8]
+        winds += in_refs[slot][2 * comps + size :].astype(F32)
+
+    first, second = winds[:8], winds[8:]
+    outer = pltpu.roll(first, 3, 0)
+
+    def joined(tile):
+        return tile[:1] + tile[1:2]
+
+    surface = jnp.concatenate([joined(first), joined(second), joined(outer)], axis=1)
+    sea = jnp.concatenate([first[2:3], second[2:3], outer[2:3]], axis=1)
+    below = jnp.concatenate([joined(first[3:5]), joined(second[3:5])], axis=1)
+    wind = surface * surface
 
     def renew(values, products, growth, wind, sea):
         half = values.shape[1]
         paired, quad_square = products[:, :half], products[:, half:]
-        return (
-            (values + 0.3 * (values * paired - quad_square) + growth * wind)
-            / (1.0 + 0.1 * values * values)
-        ) * sea
+        below = 1.0 + 0.1 * values * values
+        inverse = pl.reciprocal(below, approx=True)
+        inverse = inverse * (2.0 - below * inverse)
+        return (values + 0.3 * (values * paired - quad_square) + growth * wind) * inverse * sea
 
     part = total // 3
     for step in range(3):
@@ -328,7 +392,7 @@
         span = pl.ds(pl.multiple_of(step * part, part), part)
         products = jnp.dot(quartet_ref[span, :], first_in[...], preferred_element_type=F32)
         values = first_in[span, :wide].astype(F32)
-        fresh[span, :] = renew(values, products, growth_ref[span, :1], wind, sea).astype(BF16)
+        fresh[span, :] = renew(values, products, factors[span, 8:9], wind, sea).astype(BF16)
 
     level = lax.broadcasted_iota(jnp.int32, (2 * levels, wide), 0)
     forced = jnp.dot(coupler_ref[...], fresh[...], preferred_element_type=F32)
@@ -338,8 +402,8 @@
         first, second = values[:, :LANES], values[:, LANES:cells]
         west, east = column_neighbours(first, second, values[:, cells:], rows)
         lane = lane_of(first.shape)
-        west_edge = (base == 0) & (lane < rows)
-        east_edge = (base + width == grid_columns) & (lane >= LANES - rows)
+        west_edge = west_end & (lane < rows)
+        east_edge = east_end & (lane >= LANES - rows)
         west = (jnp.where(west_edge, 0.0, west[0]), west[1])
         east = (east[0], jnp.where(east_edge, 0.0, east[1]))
         sums = [
@@ -350,9 +414,9 @@
 
     eight = jnp.broadcast_to(surface, (8, wide))
     calm = surface[:, :cells] + 0.1 * beside(eight)[:1]
-    calm = calm + 0.1 * (below[:, :cells] - 2.0 * surface[:, :cells])
+    calm = calm + 0.1 * (below - 2.0 * surface[:, :cells])
     later = calm + forced[:1, :cells] - forced[levels : levels + 1, :cells]
-    later = 0.1 * later * later
+    later = later * later
     middle = forced[:, :cells]
     level = level[:, :cells] % levels
     above = jnp.where(level == 0, 0.0, pltpu.roll(middle, 1, 0))
@@ -366,8 +430,8 @@
         first = fresh[span, :LANES].astype(F32)
         second = fresh[span, LANES:cells].astype(F32)
         west, east = column_neighbours(first, second, fresh[span, cells:].astype(F32), rows)
-        cx = jnp.broadcast_to(growth_ref[span, 1:2], first.shape)
-        cy = jnp.broadcast_to(growth_ref[span, 2:3], first.shape)
+        cx = jnp.broadcast_to(factors[span, 0:1], first.shape)
+        cy = jnp.broadcast_to(factors[span, 2:3], first.shape)
         for i, here in enumerate((first, second)):
             moved = here - upwind(here, cx, west[i], east[i])
             moved = moved - upwind(
@@ -387,7 +451,7 @@
         span = pl.ds(pl.multiple_of(step * part, part), part)
         products = jnp.dot(quartet_ref[span, :], second_in[...], preferred_element_type=F32)
         values = second_in[span, :cells].astype(F32)
-        done = renew(values, products, growth_ref[span, :1], later, sea[:, :cells]).astype(BF16)
+        done = renew(values, products, factors[span, 8:9], later, sea[:, :cells]).astype(BF16)
         last[span, :] = done
         ordered[span, :] = jnp.dot(done, back, preferred_element_type=F32).astype(BF16)
 
@@ -419,13 +483,13 @@
     return lax.broadcasted_iota(jnp.int32, (2 * levels, cells), 0) < levels
 
 
-def finish_kernel(count, where_ref, calm_ref, *refs):
+def finish_kernel(count, calm_ref, *refs):
     in_refs, refs = refs[:count], refs[count:]
     energy_ref, air_ref, ocean_ref, pieces, wide, narrow = refs
     comps, rows, columns = energy_ref.shape
     levels, tile_rows, _ = air_ref.shape
     unit = columns // count
-    me = where_ref[0]
+    me = lax.axis_index(("cells", "lev"))
     part = 16
     for slot in range(count):
         pieces[lax.rem(me - slot + count, count)] = in_refs[slot][...]
@@ -504,61 +568,48 @@
     width = columns // count
     cells = rows * width
     levels_own, tile_rows, _ = atmosphere.shape
-    groups = max(n for n in range(1, 5) if comps % (16 * n) == 0)
-    me = lax.axis_index(axes)
-    sect = lax.axis_index("sect")
-    where = jnp.stack([me, sect * columns + me * width]).astype(jnp.int32)
+    groups = 3 if comps % 48 == 0 else 2
     params = pltpu.CompilerParams(vmem_limit_bytes=40 * 1024 * 1024)
     whole = pl.BlockSpec(memory_space=VMEM)
-    scalars = pl.BlockSpec(memory_space=pltpu.SMEM)
-
-    surface = jnp.stack(
-        [atmosphere[0] - ocean_state[0], atmosphere[1] - ocean_state[1], sea_mask.astype(F32)]
-    )
-    surface = lax.all_gather(surface, ("sect",) + axes)
-    surface = surface.reshape(sects, lax.axis_size("cells"), lax.axis_size("lev"), 3, tile_rows, columns)
-    surface = surface[:, :, 0].transpose(2, 1, 3, 0, 4).reshape(3 * rows, sects * columns)
-
-    by_row, edge = pl.pallas_call(
+
+    edge = jax.ShapeDtypeStruct((comps + 16, LANES), BF16)
+    by_row, edge, below = pl.pallas_call(
         edges_kernel,
         out_shape=(
             jax.ShapeDtypeStruct((rows, comps, columns), BF16),
-            jax.ShapeDtypeStruct((comps, LANES), BF16),
+            edge,
+            jax.ShapeDtypeStruct((16, LANES), BF16),
         ),
-        in_specs=[whole],
-        out_specs=(whole, whole),
+        in_specs=[whole] * 4,
+        out_specs=(whole,) * 3,
         scratch_shapes=[VMEM((comps * rows, columns), F32)],
         compiler_params=params,
         name="edges",
-    )(spectrum)
-    forward = [(i, (i + 1) % sects) for i in range(sects)]
-    backward = [(target, source) for source, target in forward]
-    if sects == 2:
-        halo = lax.ppermute(edge, "sect", forward)
-    else:
-        low = lax.ppermute(edge, "sect", forward)
-        high = lax.ppermute(edge, "sect", backward)
-        halo = jnp.concatenate([low[:, : LANES // 2], high[:, LANES // 2 :]], axis=1)
-
-    column_x, column_y = courant_x[:, None], courant_y[:, None]
-    piece = jax.ShapeDtypeStruct((2 * comps + comps // groups, LANES), BF16)
+    )(spectrum, atmosphere, ocean_state, sea_mask)
+    halo = lax.ppermute(edge, "sect", [(0, 1), (1, 0)])
+
+    piece = jax.ShapeDtypeStruct((2 * comps + comps // groups + 16, LANES), BF16)
     pieces = pl.pallas_call(
         functools.partial(advect_kernel, groups, count),
         out_shape=(piece,) * count,
-        in_specs=[scalars] + [whole] * 5,
+        in_specs=[whole] * 6,
         out_specs=(whole,) * count,
-        scratch_shapes=[VMEM((count,) + piece.shape, BF16), VMEM((total, cells), BF16)],
+        scratch_shapes=[
+            VMEM((count,) + piece.shape, BF16),
+            VMEM((total, cells), BF16),
+            VMEM((comps, LANES), F32),
+            VMEM((comps, LANES), F32),
+        ],
         compiler_params=params,
         name="advect",
-    )(where, by_row, edge, halo, column_x, column_y)
+    )(by_row, edge, below, halo, courant_x[None], courant_y[None])
     received = spread_out(pieces, axes, count)
 
-    factors = jnp.stack([growth, lax.all_gather(courant_x, axes, tiled=True), lax.all_gather(courant_y, axes, tiled=True)], axis=1)
     result = jax.ShapeDtypeStruct((2 * comps + levels_own, LANES), BF16)
     results = pl.pallas_call(
-        functools.partial(steps_kernel, groups, count),
+        functools.partial(steps_kernel, groups, count, rows),
         out_shape=(result,) * count,
-        in_specs=[scalars] + [whole] * (4 + count),
+        in_specs=[whole] * (3 + count),
         out_specs=(whole,) * count,
         scratch_shapes=[
             VMEM((total, 6 * LANES), BF16),
@@ -567,14 +618,15 @@
             VMEM((total, cells), BF16),
             VMEM((total, cells), BF16),
             VMEM((count, levels_own, LANES), BF16),
+            VMEM((total, LANES), F32),
         ],
         compiler_params=params,
         name="steps",
-    )(where, quartet, coupler, factors, surface, *received)
+    )(quartet, coupler, growth[None], *received)
     returned = spread_out(results, axes, count)
 
-    state = jnp.stack([atmosphere, ocean_state])
-    calm = twice_relaxed(state)
+    atmosphere, ocean_state, _ = lax.optimization_barrier((atmosphere, ocean_state, pieces[0]))
+    calm = twice_relaxed(jnp.stack([atmosphere, ocean_state]))
     return pl.pallas_call(
         functools.partial(finish_kernel, count),
         out_shape=(
@@ -582,7 +634,7 @@
             jax.ShapeDtypeStruct(atmosphere.shape, F32),
             jax.ShapeDtypeStruct(ocean_state.shape, F32),
         ),
-        in_specs=[scalars] + [whole] * (1 + count),
+        in_specs=[whole] * (1 + count),
         out_specs=(whole,) * 3,
         scratch_shapes=[
             VMEM((count,) + result.shape, BF16),
@@ -591,7 +643,7 @@
         ],
         compiler_params=params,
         name="finish",
-    )(where, calm, *returned)
+    )(calm, *returned)
 
 
 def on_device(spectrum, *rest):
@@ -601,9 +653,10 @@
     fits = (
         columns == LANES
         and blocks == 8
+        and lax.axis_size("sect") == 2
         and rows * (columns // blocks) == 2 * LANES
         and atmosphere.shape[1] * (columns // blocks) * 2 == LANES
-        and comps % 16 == 0
+        and any(comps % (16 * groups) == 0 for groups in (3, 2))
         and atmosphere.shape[0] % 16 == 0
         and NSTEP == 2
     )

time: 140 us -> 86.7 us (0.62)
  the two profiles are of different devices: /device:TPU:9 before, /device:TPU:0 now
where the time goes in v2:
time: 86.7 us; the launch traced here: 85.1 us
  starting transfers between devices  30.6 us (35%)
  Pallas kernels  20.1 us (23%)
  waiting for transfers between devices  17.8 us (21%)
  local copies, waits for them, and re-layouts  10 us (12%)
  other arithmetic  5.72 us (7%)
    ppermute x14, starting transfers between devices, spread_out(): received.append(lax.ppermute(pieces[shift], axes, pairs))  20.7 us
    pallas_call x1, Pallas kernels, by_columns(): pl.pallas_call(functools.partial(steps_kernel, groups, count, rows), out_...  12.5 us
    ppermute x14, waiting for transfers between devices, spread_out(): received.append(lax.ppermute(pieces[shift], axes, pairs))  10.2 us
    unnamed x40, local copies, waits for them, and re-layouts  9.27 us
    ppermute x1, waiting for transfers between devices, extended_2(): lax.ppermute(lax.slice_in_dim(block, 0, width, axis=dim), axis, backward)  4.29 us
    ppermute x1, starting transfers between devices, extended_2(): lax.ppermute(lax.slice_in_dim(block, block.shape[dim] - width, None, axis...  4.02 us
    pallas_call x1, Pallas kernels, by_columns(): pl.pallas_call(functools.partial(advect_kernel, groups, count), out_shape...  3.75 us
    pallas_call x1, Pallas kernels, by_columns(): pl.pallas_call(functools.partial(finish_kernel, count), out_shape=(jax.Sh...  3.27 us
  transfers between devices with their start and end apart: 19, of which 10 were waited for; matrix products, arithmetic and copies ran while one was open for 4% of the time, Pallas kernels for 0%

profile of v2, /device:TPU:0, one launch (start us, length us, event | category | flops | bytes accessed | tf_op | source)
XLA Modules:
  0.0 85.1 jit_solution(2629721219027176658)
XLA Ops:
  0.6 0.8 copy-done.1
  1.5 0.8 copy-done.3
  2.3 1.1 %copy-done.5 = bf16[144,16,128]{2,1,0:T(8,128)(2,1)S(1)} copy-done((bf16[144,16,128]{2,1,0:T(8,128)(2,1)S(1)}, bf16[144,16,128]{2,1,0:T(8,128)(2,1)}, u32[]{:S(2)}) %copy-start.5) | copy-done | bytes 589848
  4.6 3.0 %collective-permute-start = (bf16[160,128]{1,0:T(8,128)(2,1)S(1)}, bf16[160,128]{1,0:T(8,128)(2,1)S(1)}, u32[]{:S(2)}, u32[]{:S(2)}) collective-permute-start(bf16[160,128]{1,0:T(8,128)(2,1)S(1)} %get-tuple-element.25.edge_ref), channel_id=1, source_target_pairs={{0,2},{2,0},{1,3},{3,1},{4,6},{6,4},{5,7},{7,5},{8,10},{10,8},{9,1... | collective-permute-start | bytes 122888 | tf_op jit(solution)/shard_map/ppermute | solution.py:589
  7.6 2.0 %collective-permute-done.halo_ref = bf16[160,128]{1,0:T(8,128)(2,1)S(1)} collective-permute-done((bf16[160,128]{1,0:T(8,128)(2,1)S(1)}, bf16[160,128]{1,0:T(8,128)(2,1)S(1)}, u32[]{:S(2)}, u32[]{:S(2)}) %collective-permute-start) | collective-permute-done | bytes 40992 | tf_op jit(solution)/shard_map/ppermute | solution.py:589
  11.0 3.8 %advect.1 = (bf16[352,128]{1,0:T(8,128)(2,1)S(1)}, bf16[352,128]{1,0:T(8,128)(2,1)S(1)}, bf16[352,128]{1,0:T(8,128)(2,1)S(1)}, bf16[352,128]{1,0:T(8,128)(2,1)S(...) custom-call(bf16[16,144,128]{2,1,0:T(8,128)(2,1)S(1)} %get-tuple-ele, ...), custom_call_target="tpu_custom_call" | custom-call | tf_op jit(solution)/shard_map/advect/pallas_call | solution.py:592
  19.2 0.8 fusion.17
  21.2 0.9 %pad_maximum_fusion.14 = f32[2,36,4,128]{3,2,1,0:T(4,128)S(1)} fusion(f32[2,2,4,128]{3,2,1,0:T(4,128)S(1)} %get-tuple-element.50, f32[1,32,4,128]{3,2,1,0:T(4,128)} %bitcast.5, f32[1,32,4,128]{3,2,1,0:T(4,128)} %bitcast.10, f32[2,2,4,128]{3,2,1,0:T(4,128)S(1)} %get-tuple-element.49), kind=kLoop, calls=%fused_computation.28 | loop fusion | flops 110592 | bytes 294912 | tf_op jit(solution)/shard_map/concatenate | solution.py:536
  22.2 4.0 %collective-permute-start.2 = (f32[2,36,2,128]{3,2,1,0:T(2,128)S(1)}, f32[2,36,2,128]{3,2,1,0:T(2,128)S(1)}, u32[]{:S(2)}, u32[]{:S(2)}) collective-permute-start(f32[2,36,2,128]{3,2,1,0:T(2,128)S(1)} %get-tuple-element.47), channel_id=1, source_target_pairs={{0,4},{4,8},{8,12},{1,5},{5,9},{9,13},{2,6},{6,10},{10,14},{3,7},{... | collective-permute-start | bytes 221192 | tf_op jit(solution)/shard_map/ppermute | solution.py:29
  26.2 1.3 %collective-permute-start.3 = (f32[2,36,2,128]{3,2,1,0:T(2,128)S(1)}, f32[2,36,2,128]{3,2,1,0:T(2,128)S(1)}, u32[]{:S(2)}, u32[]{:S(2)}) collective-permute-start(f32[2,36,2,128]{3,2,1,0:T(2,128)S(1)} %get-tuple-element.48), channel_id=1, source_target_pairs={{4,0},{8,4},{12,8},{5,1},{9,5},{13,9},{6,2},{10,6},{14,10},{7,3},{... | collective-permute-start | bytes 221192 | tf_op jit(solution)/shard_map/ppermute | solution.py:32
  28.2 4.3 %collective-permute-done.3 = f32[2,36,2,128]{3,2,1,0:T(2,128)S(1)} collective-permute-done((f32[2,36,2,128]{3,2,1,0:T(2,128)S(1)}, f32[2,36,2,128]{3,2,1,0:T(2,128)S(1)}, u32[]{:S(2)}, u32[]{:S(2)}) %collective-permute-start.3) | collective-permute-done | bytes 73760 | tf_op jit(solution)/shard_map/ppermute | solution.py:32
  32.4 1.0 %pad_maximum_fusion.13 = f32[2,36,8,128]{3,2,1,0:T(8,128)S(1)} fusion(f32[2,36,2,128]{3,2,1,0:T(2,128)S(1)} %collective-permute-done.3, f32[2,2,4,128]{3,2,1,0:T(4,128)S(1)} %get-tuple-element.50, f32[1,32,4,128]{3,2,1,0:T(4,128)} %bitcast.6, f32[1,32,4,128]{3,2,1,0:T(4,128)} %bitcast.11, f32[2,2,4,128]{3,2,1,0:T(4,128)S(1)} %get-tuple-element.49, ...), kind=kLoop, calls=%fused_computation.27 | loop fusion | flops 368640 | bytes 589824 | tf_op jit(solution)/shard_map/concatenate | solution.py:33
  33.6 1.6 %collective-permute-start.4 = (f32[2,36,8,2]{3,2,1,0:T(8,128)S(1)}, f32[2,36,8,2]{3,2,1,0:T(8,128)S(1)}, u32[]{:S(2)}, u32[]{:S(2)}) collective-permute-start(f32[2,36,8,2]{3,2,1,0:T(8,128)S(1)} %slice_select_fusion), channel_id=1, source_target_pairs={{0,2},{2,0},{1,3},{3,1},{4,6},{6,4},{5,7},{7,5},{8,10},{10,8},{9,1... | collective-permute-start | bytes 13832 | tf_op jit(solution)/shard_map/ppermute | solution.py:533
  35.1 0.7 broadcast_in_dim.32.growth_ref
  35.8 1.6 %collective-permute-start.6 = (bf16[352,128]{1,0:T(8,128)(2,1)}, bf16[352,128]{1,0:T(8,128)(2,1)S(1)}, u32[]{:S(2)}, u32[]{:S(2)}) collective-permute-start(bf16[352,128]{1,0:T(8,128)(2,1)} %copy-done.17), channel_id=1, source_target_pairs={{0,4},{1,5},{4,8},{5,9},{8,12},{9,13},{12,0},{13,1},{2,6},{3,7},{6... | collective-permute-start | bytes 270344 | tf_op jit(solution)/shard_map/ppermute | solution.py:556
  37.4 1.3 %collective-permute-start.7 = (bf16[352,128]{1,0:T(8,128)(2,1)}, bf16[352,128]{1,0:T(8,128)(2,1)S(1)}, u32[]{:S(2)}, u32[]{:S(2)}) collective-permute-start(bf16[352,128]{1,0:T(8,128)(2,1)} %copy-done.16), channel_id=1, source_target_pairs={{0,5},{1,8},{4,9},{5,12},{8,13},{9,0},{12,1},{13,4},{2,7},{3,10},{... | collective-permute-start | bytes 270344 | tf_op jit(solution)/shard_map/ppermute | solution.py:556
  38.7 2.5 %collective-permute-start.8 = (bf16[352,128]{1,0:T(8,128)(2,1)}, bf16[352,128]{1,0:T(8,128)(2,1)S(1)}, u32[]{:S(2)}, u32[]{:S(2)}) collective-permute-start(bf16[352,128]{1,0:T(8,128)(2,1)} %copy-done.15), channel_id=1, source_target_pairs={{0,8},{1,9},{4,12},{5,13},{8,0},{9,1},{12,4},{13,5},{2,10},{3,11},... | collective-permute-start | bytes 270344 | tf_op jit(solution)/shard_map/ppermute | solution.py:556
  41.3 0.9 %collective-permute-done.5.refs_1_ = bf16[352,128]{1,0:T(8,128)(2,1)S(1)} collective-permute-done((bf16[352,128]{1,0:T(8,128)(2,1)}, bf16[352,128]{1,0:T(8,128)(2,1)S(1)}, u32[]{:S(2)}, u32[]{:S(2)}) %collective-permute-start.5) | collective-permute-done | bytes 90144 | tf_op jit(solution)/shard_map/ppermute | solution.py:556
  42.3 1.6 %collective-permute-start.10 = (bf16[352,128]{1,0:T(8,128)(2,1)S(1)}, bf16[352,128]{1,0:T(8,128)(2,1)S(1)}, u32[]{:S(2)}, u32[]{:S(2)}) collective-permute-start(bf16[352,128]{1,0:T(8,128)(2,1)S(1)} %copy-done.13), channel_id=1, source_target_pairs={{0,12},{1,13},{4,0},{5,1},{8,4},{9,5},{12,8},{13,9},{2,14},{3,15},... | collective-permute-start | bytes 270344 | tf_op jit(solution)/shard_map/ppermute | solution.py:556
  43.9 1.5 %collective-permute-start.11 = (bf16[352,128]{1,0:T(8,128)(2,1)S(1)}, bf16[352,128]{1,0:T(8,128)(2,1)S(1)}, u32[]{:S(2)}, u32[]{:S(2)}) collective-permute-start(bf16[352,128]{1,0:T(8,128)(2,1)S(1)} %copy-done.11), channel_id=1, source_target_pairs={{0,13},{1,0},{4,1},{5,4},{8,5},{9,8},{12,9},{13,12},{2,15},{3,2},{... | collective-permute-start | bytes 270344 | tf_op jit(solution)/shard_map/ppermute | solution.py:556
  46.0 4.5 %collective-permute-done.7.refs_3_ = bf16[352,128]{1,0:T(8,128)(2,1)S(1)} collective-permute-done((bf16[352,128]{1,0:T(8,128)(2,1)}, bf16[352,128]{1,0:T(8,128)(2,1)S(1)}, u32[]{:S(2)}, u32[]{:S(2)}) %collective-permute-start.7) | collective-permute-done | bytes 90144 | tf_op jit(solution)/shard_map/ppermute | solution.py:556
  50.7 12.5 %steps.1 = (bf16[320,128]{1,0:T(8,128)(2,1)S(1)}, bf16[320,128]{1,0:T(8,128)(2,1)S(1)}, bf16[320,128]{1,0:T(8,128)(2,1)S(1)}, bf16[320,128]{1,0:T(8,128)(2,1)S(1...) custom-call(bf16[1152,1152]{1,0:T(8,128)(2,1)S(1)} %copy-done, ...), custom_call_target="tpu_custom_call" | custom-call | tf_op jit(solution)/shard_map/steps/pallas_call | solution.py:609
  63.3 2.0 %collective-permute-start.12 = (bf16[320,128]{1,0:T(8,128)(2,1)S(1)}, bf16[320,128]{1,0:T(8,128)(2,1)S(1)}, u32[]{:S(2)}, u32[]{:S(2)}) collective-permute-start(bf16[320,128]{1,0:T(8,128)(2,1)S(1)} %get-tuple-element.38), channel_id=1, source_target_pairs={{0,1},{1,4},{4,5},{5,8},{8,9},{9,12},{12,13},{13,0},{2,3},{3,6},{6... | collective-permute-start | bytes 245768 | tf_op jit(solution)/shard_map/ppermute | solution.py:556
  65.3 4.0 %collective-permute-start.13 = (bf16[320,128]{1,0:T(8,128)(2,1)S(1)}, bf16[320,128]{1,0:T(8,128)(2,1)S(1)}, u32[]{:S(2)}, u32[]{:S(2)}) collective-permute-start(bf16[320,128]{1,0:T(8,128)(2,1)S(1)} %get-tuple-element.39), channel_id=1, source_target_pairs={{0,4},{1,5},{4,8},{5,9},{8,12},{9,13},{12,0},{13,1},{2,6},{3,7},{6... | collective-permute-start | bytes 245768 | tf_op jit(solution)/shard_map/ppermute | solution.py:556
  69.3 1.3 %fusion.5 = f32[2,34,6,130]{3,2,1,0:T(8,128)S(1)} fusion(f32[2,36,8,132]{3,2,1,0:T(8,128)S(1)} %pad_maximum_fusion, f32[2,36,8,2]{3,2,1,0:T(8,128)S(1)} %get-tuple-element.45, f32[2,36,2,128]{3,2,1,0:T(2,128)S(1)} %collective-permute-done.3, f32[2,36,2,128]{3,2,1,0:T(2,128)S(1)} %collective-permute-done.2, f32[2,2,4,128]{3,2,1,0:T(4,128)S(1)} %get-tuple-element.50, ...), kind=kLoop, calls=%fused_computation.7 | loop fusion | flops 1432080 | bytes 1577258 | tf_op jit(solution)/shard_map/jit(_where)/select_n | solution.py:548
  71.1 1.9 %collective-permute-start.15 = (bf16[320,128]{1,0:T(8,128)(2,1)S(1)}, bf16[320,128]{1,0:T(8,128)(2,1)S(1)}, u32[]{:S(2)}, u32[]{:S(2)}) collective-permute-start(bf16[320,128]{1,0:T(8,128)(2,1)S(1)} %get-tuple-element.41), channel_id=1, source_target_pairs={{0,8},{1,9},{4,12},{5,13},{8,0},{9,1},{12,4},{13,5},{2,10},{3,11},... | collective-permute-start | bytes 245768 | tf_op jit(solution)/shard_map/ppermute | solution.py:556
  73.0 1.6 %collective-permute-start.16 = (bf16[320,128]{1,0:T(8,128)(2,1)S(1)}, bf16[320,128]{1,0:T(8,128)(2,1)S(1)}, u32[]{:S(2)}, u32[]{:S(2)}) collective-permute-start(bf16[320,128]{1,0:T(8,128)(2,1)S(1)} %get-tuple-element.42), channel_id=1, source_target_pairs={{0,9},{1,12},{4,13},{5,0},{8,1},{9,4},{12,5},{13,8},{2,11},{3,14},... | collective-permute-start | bytes 245768 | tf_op jit(solution)/shard_map/ppermute | solution.py:556
  75.4 1.4 %collective-permute-start.18 = (bf16[320,128]{1,0:T(8,128)(2,1)S(1)}, bf16[320,128]{1,0:T(8,128)(2,1)S(1)}, u32[]{:S(2)}, u32[]{:S(2)}) collective-permute-start(bf16[320,128]{1,0:T(8,128)(2,1)S(1)} %get-tuple-element.44), channel_id=1, source_target_pairs={{0,13},{1,0},{4,1},{5,4},{8,5},{9,8},{12,9},{13,12},{2,15},{3,2},{... | collective-permute-start | bytes 245768 | tf_op jit(solution)/shard_map/ppermute | solution.py:556
  77.3 1.0 %collective-permute-done.14.refs_3_ = bf16[320,128]{1,0:T(8,128)(2,1)S(1)} collective-permute-done((bf16[320,128]{1,0:T(8,128)(2,1)S(1)}, bf16[320,128]{1,0:T(8,128)(2,1)S(1)}, u32[]{:S(2)}, u32[]{:S(2)}) %collective-permute-start.14) | collective-permute-done | bytes 81952 | tf_op jit(solution)/shard_map/ppermute | solution.py:556
  78.3 2.5 %collective-permute-done.15.refs_4_ = bf16[320,128]{1,0:T(8,128)(2,1)S(1)} collective-permute-done((bf16[320,128]{1,0:T(8,128)(2,1)S(1)}, bf16[320,128]{1,0:T(8,128)(2,1)S(1)}, u32[]{:S(2)}, u32[]{:S(2)}) %collective-permute-start.15) | collective-permute-done | bytes 81952 | tf_op jit(solution)/shard_map/ppermute | solution.py:556
  80.7 1.1 %collective-permute-done.17.refs_6_ = bf16[320,128]{1,0:T(8,128)(2,1)S(1)} collective-permute-done((bf16[320,128]{1,0:T(8,128)(2,1)S(1)}, bf16[320,128]{1,0:T(8,128)(2,1)S(1)}, u32[]{:S(2)}, u32[]{:S(2)}) %collective-permute-start.17) | collective-permute-done | bytes 81952 | tf_op jit(solution)/shard_map/ppermute | solution.py:556
  81.8 3.3 %finish.1 = (bf16[144,16,128]{2,1,0:T(8,128)(2,1)}, f32[32,4,128]{2,1,0:T(4,128)}, f32[32,4,128]{2,1,0:T(4,128)}) custom-call(f32[2,32,4,128]{3,2,1,0:T(4,128)S(1)} %fusion.13.calm_ref, bf16[320,128]{1,0:T(8,128)(2,1)S(1)} %get-tuple-element.37.refs_0_, bf16[320,128]{1,0:T(8,128)(2,1)S(1)} %collective-permute-done.12.refs_1_, ...), custom_call_target="tpu_custom_call" | custom-call | tf_op jit(solution)/shard_map/finish/pallas_call | solution.py:630
  (64 shorter events, 11.8 us)
Async XLA Ops:
  0.6 0.8 copy-start.1
  1.5 0.8 copy-start.3
  2.3 1.1 %copy-start.5 = (bf16[144,16,128]{2,1,0:T(8,128)(2,1)S(1)}, bf16[144,16,128]{2,1,0:T(8,128)(2,1)}, u32[]{:S(2)}) copy-start(bf16[144,16,128]{2,1,0:T(8,128)(2,1)} %x_ref.1) | copy-start | bytes 1769476
  3.4 0.7 copy-start.7
  4.1 41.3 %copy-start.2 = (f32[32,4,128]{2,1,0:T(4,128)S(1)}, f32[32,4,128]{2,1,0:T(4,128)}, u32[]{:S(2)}) copy-start(f32[32,4,128]{2,1,0:T(4,128)} %ocean_ref.1) | copy-start | bytes 196612
  4.1 41.3 %copy-start.4 = (f32[32,4,128]{2,1,0:T(4,128)S(1)}, f32[32,4,128]{2,1,0:T(4,128)}, u32[]{:S(2)}) copy-start(f32[32,4,128]{2,1,0:T(4,128)} %air_ref.1) | copy-start | bytes 196612
  4.6 5.0 %collective-permute-start = (bf16[160,128]{1,0:T(8,128)(2,1)S(1)}, bf16[160,128]{1,0:T(8,128)(2,1)S(1)}, u32[]{:S(2)}, u32[]{:S(2)}) collective-permute-start(bf16[160,128]{1,0:T(8,128)(2,1)S(1)} %get-tuple-element.25.edge_ref), channel_id=1, source_target_pairs={{0,2},{2,0},{1,3},{3,1},{4,6},{6,4},{5,7},{7,5},{8,10},{10,8},{9,1... | collective-permute-start | bytes 122888 | tf_op jit(solution)/shard_map/ppermute | solution.py:589
  9.6 0.7 copy-start.8
  10.3 0.7 copy-start.9
  11.0 39.7 %copy-start = (bf16[1152,1152]{1,0:T(8,128)(2,1)S(1)}, bf16[1152,1152]{1,0:T(8,128)(2,1)}, u32[]{:S(2)}) copy-start(bf16[1152,1152]{1,0:T(8,128)(2,1)} %quartet_ref.1) | copy-start | bytes 7962628
  18.6 32.1 %copy-start.6 = (bf16[128,1152]{1,0:T(8,128)(2,1)S(1)}, bf16[128,1152]{1,0:T(8,128)(2,1)}, u32[]{:S(2)}) copy-start(bf16[128,1152]{1,0:T(8,128)(2,1)} %coupler_ref.1) | copy-start | bytes 884740
  19.2 24.7 %copy-start.11 = (bf16[352,128]{1,0:T(8,128)(2,1)S(1)}, bf16[352,128]{1,0:T(8,128)(2,1)}, u32[]{:S(2)}) copy-start(bf16[352,128]{1,0:T(8,128)(2,1)} %copy-done.10) | copy-start | bytes 270340
  20.0 1.2 %collective-permute-start.1 = (f32[2,2,4,128]{3,2,1,0:T(4,128)S(1)}, f32[2,2,4,128]{3,2,1,0:T(4,128)S(1)}, u32[]{:S(2)}, u32[]{:S(2)}) collective-permute-start(f32[2,2,4,128]{3,2,1,0:T(4,128)S(1)} %fusion.17), channel_id=1, source_target_pairs={{0,1},{1,0},{2,3},{3,2},{4,5},{5,4},{6,7},{7,6},{8,9},{9,8},{10,11... | collective-permute-start | bytes 24584 | tf_op jit(solution)/shard_map/ppermute | solution.py:533
  20.6 21.7 %copy-start.13 = (bf16[352,128]{1,0:T(8,128)(2,1)S(1)}, bf16[352,128]{1,0:T(8,128)(2,1)}, u32[]{:S(2)}) copy-start(bf16[352,128]{1,0:T(8,128)(2,1)} %copy-done.12) | copy-start | bytes 270340
  22.2 6.0 %collective-permute-start.2 = (f32[2,36,2,128]{3,2,1,0:T(2,128)S(1)}, f32[2,36,2,128]{3,2,1,0:T(2,128)S(1)}, u32[]{:S(2)}, u32[]{:S(2)}) collective-permute-start(f32[2,36,2,128]{3,2,1,0:T(2,128)S(1)} %get-tuple-element.47), channel_id=1, source_target_pairs={{0,4},{4,8},{8,12},{1,5},{5,9},{9,13},{2,6},{6,10},{10,14},{3,7},{... | collective-permute-start | bytes 221192 | tf_op jit(solution)/shard_map/ppermute | solution.py:29
  26.2 6.2 %collective-permute-start.3 = (f32[2,36,2,128]{3,2,1,0:T(2,128)S(1)}, f32[2,36,2,128]{3,2,1,0:T(2,128)S(1)}, u32[]{:S(2)}, u32[]{:S(2)}) collective-permute-start(f32[2,36,2,128]{3,2,1,0:T(2,128)S(1)} %get-tuple-element.48), channel_id=1, source_target_pairs={{4,0},{8,4},{12,8},{5,1},{9,5},{13,9},{6,2},{10,6},{14,10},{7,3},{... | collective-permute-start | bytes 221192 | tf_op jit(solution)/shard_map/ppermute | solution.py:32
  33.6 7.7 %collective-permute-start.4 = (f32[2,36,8,2]{3,2,1,0:T(8,128)S(1)}, f32[2,36,8,2]{3,2,1,0:T(8,128)S(1)}, u32[]{:S(2)}, u32[]{:S(2)}) collective-permute-start(f32[2,36,8,2]{3,2,1,0:T(8,128)S(1)} %slice_select_fusion), channel_id=1, source_target_pairs={{0,2},{2,0},{1,3},{3,1},{4,6},{6,4},{5,7},{7,5},{8,10},{10,8},{9,1... | collective-permute-start | bytes 13832 | tf_op jit(solution)/shard_map/ppermute | solution.py:533
  35.8 6.4 %collective-permute-start.5 = (bf16[352,128]{1,0:T(8,128)(2,1)}, bf16[352,128]{1,0:T(8,128)(2,1)S(1)}, u32[]{:S(2)}, u32[]{:S(2)}) collective-permute-start(bf16[352,128]{1,0:T(8,128)(2,1)} %copy-done.18), channel_id=1, source_target_pairs={{0,1},{1,4},{4,5},{5,8},{8,9},{9,12},{12,13},{13,0},{2,3},{3,6},{6... | collective-permute-start | bytes 270344 | tf_op jit(solution)/shard_map/ppermute | solution.py:556
  35.8 8.1 %collective-permute-start.6 = (bf16[352,128]{1,0:T(8,128)(2,1)}, bf16[352,128]{1,0:T(8,128)(2,1)S(1)}, u32[]{:S(2)}, u32[]{:S(2)}) collective-permute-start(bf16[352,128]{1,0:T(8,128)(2,1)} %copy-done.17), channel_id=1, source_target_pairs={{0,4},{1,5},{4,8},{5,9},{8,12},{9,13},{12,0},{13,1},{2,6},{3,7},{6... | collective-permute-start | bytes 270344 | tf_op jit(solution)/shard_map/ppermute | solution.py:556
  37.4 13.0 %collective-permute-start.7 = (bf16[352,128]{1,0:T(8,128)(2,1)}, bf16[352,128]{1,0:T(8,128)(2,1)S(1)}, u32[]{:S(2)}, u32[]{:S(2)}) collective-permute-start(bf16[352,128]{1,0:T(8,128)(2,1)} %copy-done.16), channel_id=1, source_target_pairs={{0,5},{1,8},{4,9},{5,12},{8,13},{9,0},{12,1},{13,4},{2,7},{3,10},{... | collective-permute-start | bytes 270344 | tf_op jit(solution)/shard_map/ppermute | solution.py:556
  38.7 11.9 %collective-permute-start.8 = (bf16[352,128]{1,0:T(8,128)(2,1)}, bf16[352,128]{1,0:T(8,128)(2,1)S(1)}, u32[]{:S(2)}, u32[]{:S(2)}) collective-permute-start(bf16[352,128]{1,0:T(8,128)(2,1)} %copy-done.15), channel_id=1, source_target_pairs={{0,8},{1,9},{4,12},{5,13},{8,0},{9,1},{12,4},{13,5},{2,10},{3,11},... | collective-permute-start | bytes 270344 | tf_op jit(solution)/shard_map/ppermute | solution.py:556
  41.3 9.4 %collective-permute-start.9 = (bf16[352,128]{1,0:T(8,128)(2,1)}, bf16[352,128]{1,0:T(8,128)(2,1)S(1)}, u32[]{:S(2)}, u32[]{:S(2)}) collective-permute-start(bf16[352,128]{1,0:T(8,128)(2,1)} %copy-done.14), channel_id=1, source_target_pairs={{0,9},{1,12},{4,13},{5,0},{8,1},{9,4},{12,5},{13,8},{2,11},{3,14},... | collective-permute-start | bytes 270344 | tf_op jit(solution)/shard_map/ppermute | solution.py:556
  41.3 28.0 %copy-start.19 = (pred[34]{0:T(512)(128)(4,1)S(1)}, pred[34]{0:T(512)(128)(4,1)}, u32[]{:S(2)}) copy-start(pred[34]{0:T(512)(128)(4,1)} %and_or_fusion) | copy-start | bytes 106
  42.3 8.4 %collective-permute-start.10 = (bf16[352,128]{1,0:T(8,128)(2,1)S(1)}, bf16[352,128]{1,0:T(8,128)(2,1)S(1)}, u32[]{:S(2)}, u32[]{:S(2)}) collective-permute-start(bf16[352,128]{1,0:T(8,128)(2,1)S(1)} %copy-done.13), channel_id=1, source_target_pairs={{0,12},{1,13},{4,0},{5,1},{8,4},{9,5},{12,8},{13,9},{2,14},{3,15},... | collective-permute-start | bytes 270344 | tf_op jit(solution)/shard_map/ppermute | solution.py:556
  43.9 6.8 %collective-permute-start.11 = (bf16[352,128]{1,0:T(8,128)(2,1)S(1)}, bf16[352,128]{1,0:T(8,128)(2,1)S(1)}, u32[]{:S(2)}, u32[]{:S(2)}) collective-permute-start(bf16[352,128]{1,0:T(8,128)(2,1)S(1)} %copy-done.11), channel_id=1, source_target_pairs={{0,13},{1,0},{4,1},{5,4},{8,5},{9,8},{12,9},{13,12},{2,15},{3,2},{... | collective-permute-start | bytes 270344 | tf_op jit(solution)/shard_map/ppermute | solution.py:556
  63.3 11.4 %collective-permute-start.12 = (bf16[320,128]{1,0:T(8,128)(2,1)S(1)}, bf16[320,128]{1,0:T(8,128)(2,1)S(1)}, u32[]{:S(2)}, u32[]{:S(2)}) collective-permute-start(bf16[320,128]{1,0:T(8,128)(2,1)S(1)} %get-tuple-element.38), channel_id=1, source_target_pairs={{0,1},{1,4},{4,5},{5,8},{8,9},{9,12},{12,13},{13,0},{2,3},{3,6},{6... | collective-permute-start | bytes 245768 | tf_op jit(solution)/shard_map/ppermute | solution.py:556
  65.3 10.1 %collective-permute-start.13 = (bf16[320,128]{1,0:T(8,128)(2,1)S(1)}, bf16[320,128]{1,0:T(8,128)(2,1)S(1)}, u32[]{:S(2)}, u32[]{:S(2)}) collective-permute-start(bf16[320,128]{1,0:T(8,128)(2,1)S(1)} %get-tuple-element.39), channel_id=1, source_target_pairs={{0,4},{1,5},{4,8},{5,9},{8,12},{9,13},{12,0},{13,1},{2,6},{3,7},{6... | collective-permute-start | bytes 245768 | tf_op jit(solution)/shard_map/ppermute | solution.py:556
  70.6 7.7 %collective-permute-start.14 = (bf16[320,128]{1,0:T(8,128)(2,1)S(1)}, bf16[320,128]{1,0:T(8,128)(2,1)S(1)}, u32[]{:S(2)}, u32[]{:S(2)}) collective-permute-start(bf16[320,128]{1,0:T(8,128)(2,1)S(1)} %get-tuple-element.40), channel_id=1, source_target_pairs={{0,5},{1,8},{4,9},{5,12},{8,13},{9,0},{12,1},{13,4},{2,7},{3,10},{... | collective-permute-start | bytes 245768 | tf_op jit(solution)/shard_map/ppermute | solution.py:556
  71.1 9.6 %collective-permute-start.15 = (bf16[320,128]{1,0:T(8,128)(2,1)S(1)}, bf16[320,128]{1,0:T(8,128)(2,1)S(1)}, u32[]{:S(2)}, u32[]{:S(2)}) collective-permute-start(bf16[320,128]{1,0:T(8,128)(2,1)S(1)} %get-tuple-element.41), channel_id=1, source_target_pairs={{0,8},{1,9},{4,12},{5,13},{8,0},{9,1},{12,4},{13,5},{2,10},{3,11},... | collective-permute-start | bytes 245768 | tf_op jit(solution)/shard_map/ppermute | solution.py:556
  73.0 7.7 %collective-permute-start.16 = (bf16[320,128]{1,0:T(8,128)(2,1)S(1)}, bf16[320,128]{1,0:T(8,128)(2,1)S(1)}, u32[]{:S(2)}, u32[]{:S(2)}) collective-permute-start(bf16[320,128]{1,0:T(8,128)(2,1)S(1)} %get-tuple-element.42), channel_id=1, source_target_pairs={{0,9},{1,12},{4,13},{5,0},{8,1},{9,4},{12,5},{13,8},{2,11},{3,14},... | collective-permute-start | bytes 245768 | tf_op jit(solution)/shard_map/ppermute | solution.py:556
  74.7 7.2 %collective-permute-start.17 = (bf16[320,128]{1,0:T(8,128)(2,1)S(1)}, bf16[320,128]{1,0:T(8,128)(2,1)S(1)}, u32[]{:S(2)}, u32[]{:S(2)}) collective-permute-start(bf16[320,128]{1,0:T(8,128)(2,1)S(1)} %get-tuple-element.43), channel_id=1, source_target_pairs={{0,12},{1,13},{4,0},{5,1},{8,4},{9,5},{12,8},{13,9},{2,14},{3,15},... | collective-permute-start | bytes 245768 | tf_op jit(solution)/shard_map/ppermute | solution.py:556
  75.4 6.5 %collective-permute-start.18 = (bf16[320,128]{1,0:T(8,128)(2,1)S(1)}, bf16[320,128]{1,0:T(8,128)(2,1)S(1)}, u32[]{:S(2)}, u32[]{:S(2)}) collective-permute-start(bf16[320,128]{1,0:T(8,128)(2,1)S(1)} %get-tuple-element.44), channel_id=1, source_target_pairs={{0,13},{1,0},{4,1},{5,4},{8,5},{9,8},{12,9},{13,12},{2,15},{3,2},{... | collective-permute-start | bytes 245768 | tf_op jit(solution)/shard_map/ppermute | solution.py:556
  (7 other events, 4.5 us)
